TPU v7x, 512 devices: a whole 4x4x16 slice. The times are simulated.
512 devices in a mesh: row: 8 (over z_hi, x), col: 8 (over z_lo), layer: 8 (over y, core).
Axes of the slice: x: 4, y: 4, z: 16 (z_hi: 2, z_lo: 8; z = z_hi * 8 + z_lo), core: 2. Of those that a mesh axis runs over, the one named last changes fastest.
Arguments:
- blocks: float32 [128, 8, 3, 96, 96], P(('row', 'layer'), 'col'), may hold values from -2.4 to 2.4
- block_cols: int32 [128, 8, 3], replicated, may hold values from 0 to 15, as said below
- occupancy: int32 [128, 8, 3], replicated, may hold values from 0 to 1, as said below
Outputs:
- product: float32 [128, 8, 3, 96, 96], P(('row', 'layer'), 'col')
- trace: float32 [], replicated
Inputs may be any that keep to these rules, and one draw needn't show every extreme that they name: `block_cols`: within one block row and column group the 3 block columns are distinct; for block row I the column group I // 16 holds I % 16 in slot 0. `occupancy`: slot 0 of block row I in column group I // 16 is always 1.
All inputs are finite; a program needn't handle non-finite values.
Results may differ from a plain program's by a relative error of at most 0.0003.
Values sent between devices are 32-bit elements; how exact they have to be, the bound alone decides.
A program may use at most 64 MiB of HBM per device.

v0:
```python
import jax
import jax.numpy as jnp
from jax import lax
from jax.sharding import PartitionSpec as P


def passed_along(value, axis, by):
    size = lax.axis_size(axis)
    return lax.ppermute(value, axis, [(i, (i + by) % size) for i in range(size)])


def pick_meta(table, first_row, row_count, group):
    slots = table.shape[2]
    piece = lax.dynamic_slice(table, (first_row, group, 0), (row_count, 1, slots))
    return piece[:, 0]


def local_product(left, left_cols, left_occ, right, right_cols, right_occ, out_cols, out_occ):
    gathered = jnp.take(right, left_cols, axis=0)
    inner_cols = jnp.take(right_cols, left_cols, axis=0)
    inner_occ = jnp.take(right_occ, left_cols, axis=0).astype(jnp.float32)
    match = (inner_cols[:, :, :, None] == out_cols[:, None, None, :]).astype(jnp.float32)
    match = match * inner_occ[:, :, :, None] * left_occ.astype(jnp.float32)[:, :, None, None]
    combined = jnp.einsum("itus,itubd->itsbd", match, gathered, precision=lax.Precision.HIGHEST)
    result = jnp.einsum("itab,itsbd->isad", left, combined, precision=lax.Precision.HIGHEST)
    return result * out_occ.astype(jnp.float32)[:, :, None, None]


def diagonal_sum(terms, cols_here, occ_here, first_row, group, width):
    rows = first_row + jnp.arange(terms.shape[0], dtype=jnp.int32)[:, None]
    hit = (group * width + cols_here == rows).astype(jnp.float32) * occ_here.astype(jnp.float32)
    return jnp.sum(hit * jnp.trace(terms, axis1=2, axis2=3))


def body(blocks, block_cols, occupancy):
    n_row = lax.axis_size("row")
    n_col = lax.axis_size("col")
    n_layer = lax.axis_size("layer")
    row_id = lax.axis_index("row")
    col_id = lax.axis_index("col")
    layer_id = lax.axis_index("layer")
    row_block = blocks.shape[0]
    tile_rows = row_block * n_layer
    width = row_block * n_row
    ratio = n_col // n_row
    group = (row_id + col_id + layer_id) % n_col
    tile = lax.all_gather(blocks, "layer", axis=0, tiled=True)
    left_tile = tile
    distance = (row_id + layer_id) % n_col
    for bit in range(max(n_col - 1, 0).bit_length()):
        moved = passed_along(left_tile, "col", -(1 << bit))
        left_tile = jnp.where(distance >> bit & 1 == 1, moved, left_tile)
    left = left_tile[:, 0]
    right_tile = tile
    source_row = group // ratio
    right_distance = (source_row - row_id) % n_row
    for bit in range(max(n_row - 1, 0).bit_length()):
        moved = passed_along(right_tile, "row", -(1 << bit))
        right_tile = jnp.where(right_distance >> bit & 1 == 1, moved, right_tile)
    right_rows = right_tile[:, 0]
    first_row = row_id * tile_rows
    left_cols = pick_meta(block_cols, first_row, tile_rows, group)
    left_occ = pick_meta(occupancy, first_row, tile_rows, group)
    right_cols = pick_meta(block_cols, group * width, width, col_id)
    right_occ = pick_meta(occupancy, group * width, width, col_id)
    out_cols = pick_meta(block_cols, first_row, tile_rows, col_id)
    out_occ = pick_meta(occupancy, first_row, tile_rows, col_id)
    terms = local_product(
        left, left_cols, left_occ, right_rows, right_cols, right_occ, out_cols, out_occ
    )
    summed = lax.psum_scatter(terms, "layer", scatter_dimension=0, tiled=True)
    product = summed[:, None]
    own_row = first_row + layer_id * row_block
    own_cols = pick_meta(block_cols, own_row, row_block, col_id)
    own_occ = pick_meta(occupancy, own_row, row_block, col_id)
    local_trace = diagonal_sum(summed, own_cols, own_occ, own_row, col_id, width)
    trace = lax.psum(local_trace, ("row", "col", "layer"))
    return (product, trace)


def solution(mesh):
    in_specs = (P(("row", "layer"), "col", None, None, None), P(), P())
    out_specs = (P(("row", "layer"), "col", None, None, None), P())
    return jax.shard_map(body, mesh=mesh, in_specs=in_specs, out_specs=out_specs, check_vma=False)
```

profile of v0, /device:TPU:1, one launch (start us, length us, event | category | flops | bytes accessed | tf_op | source)
XLA Modules:
  0.0 1201.4 jit_solution(12852895001826029143)
XLA Ops:
  7.2 0.7 all-gather.2.cloned.1.call-update
  7.9 41.2 %all-gather.2.cloned.1.call-done = f32[16,1,3,96,96]{4,3,2,1,0:T(8,128)} async-done(((f32[2,1,3,96,96]{4,3,2,1,0:T(8,128)}), f32[16,1,3,96,96]{4,3,2,1,0:T(8,128)}) %all-gather.2.cloned.1.call-update) | async-done | bytes 1769488 | tf_op jit(solution)/shard_map/all_gather | solution.py:47
  49.2 14.6 %collective-permute-start = (f32[16,1,3,96,96]{4,3,2,1,0:T(8,128)}, f32[16,1,3,96,96]{4,3,2,1,0:T(8,128)S(1)}, u32[]{:S(2)}, u32[]{:S(2)}) collective-permute-start(f32[16,1,3,96,96]{4,3,2,1,0:T(8,128)} %all-gather.2.cloned.1.call-done), channel_id=1, source_target_pairs={{0,448},{64,0},{128,64},{192,128},{256,192},{320,256},{384,320},{4... | collective-permute-start | bytes 5308424 | tf_op jit(solution)/shard_map/ppermute | solution.py:9
  63.8 2.8 collective-permute-start.3
  66.7 169.4 %collective-permute-done = f32[16,1,3,96,96]{4,3,2,1,0:T(8,128)S(1)} collective-permute-done((f32[16,1,3,96,96]{4,3,2,1,0:T(8,128)}, f32[16,1,3,96,96]{4,3,2,1,0:T(8,128)S(1)}, u32[]{:S(2)}, u32[]{:S(2)}) %collective-permute-start) | collective-permute-done | bytes 1769504 | tf_op jit(solution)/shard_map/ppermute | solution.py:9
  236.2 1.4 copy-done.2
  237.6 81.4 %collective-permute-done.3 = f32[16,1,3,96,96]{4,3,2,1,0:T(8,128)} collective-permute-done((f32[16,1,3,96,96]{4,3,2,1,0:T(8,128)}, f32[16,1,3,96,96]{4,3,2,1,0:T(8,128)}, u32[]{:S(2)}, u32[]{:S(2)}) %collective-permute-start.3) | collective-permute-done | bytes 1769504 | tf_op jit(solution)/shard_map/ppermute | solution.py:9
  318.9 5.2 broadcast_select_fusion.2
  324.2 1.9 collective-permute-start.1
  326.1 2.3 collective-permute-start.4
  328.4 187.5 %collective-permute-done.1 = f32[16,1,3,96,96]{4,3,2,1,0:T(8,128)} collective-permute-done((f32[16,1,3,96,96]{4,3,2,1,0:T(8,128)S(1)}, f32[16,1,3,96,96]{4,3,2,1,0:T(8,128)}, u32[]{:S(2)}, u32[]{:S(2)}) %collective-permute-start.1) | collective-permute-done | bytes 1769504 | tf_op jit(solution)/shard_map/ppermute | solution.py:9
  515.8 2.0 broadcast_select_fusion.3
  517.9 2.0 collective-permute-start.2
  520.6 314.4 %collective-permute-done.4 = f32[16,1,3,96,96]{4,3,2,1,0:T(8,128)} collective-permute-done((f32[16,1,3,96,96]{4,3,2,1,0:T(8,128)}, f32[16,1,3,96,96]{4,3,2,1,0:T(8,128)}, u32[]{:S(2)}, u32[]{:S(2)}) %collective-permute-start.4) | collective-permute-done | bytes 1769504 | tf_op jit(solution)/shard_map/ppermute | solution.py:9
  835.0 3.5 broadcast_select_fusion.1
  838.5 52.5 %collective-permute-start.5 = (f32[16,1,3,96,96]{4,3,2,1,0:T(8,128)}, f32[16,1,3,96,96]{4,3,2,1,0:T(8,128)}, u32[]{:S(2)}, u32[]{:S(2)}) collective-permute-start(f32[16,1,3,96,96]{4,3,2,1,0:T(8,128)} %broadcast_select_fusion.1), channel_id=1, source_target_pairs={{0,32},{8,40},{16,48},{24,56},{32,0},{40,8},{48,16},{56,24},{1,33}... | collective-permute-start | bytes 5308424 | tf_op jit(solution)/shard_map/ppermute | solution.py:9
  891.0 0.6 gather_fusion.1
  891.7 0.1 copy.57
  891.9 0.2 copy.61
  892.1 0.6 gather_fusion.2
  893.0 0.1 copy.67
  893.4 2.1 select_bitcast_fusion
  895.4 3.9 gather_fusion
  899.4 24.9 %fusion = f32[16,3,3,96,96]{4,2,3,1,0:T(4,128)S(1)} fusion(f32[16,3,3,96,96]{4,3,2,1,0:T(8,128)} %bitcast.45, pred[16,3]{1,0:T(8,128)(4,1)S(1)} %copy.57, f32[16,3]{1,0:T(8,128)S(1)} %bitcast.50, f32[16,3,3]{2,1,0:T(4,128)S(1)} %copy.67, s32[16,3]{1,0:T(8,128)S(1)} %bitcast.49, s32[16,3,3]{2,1,0:T(4,128)S(1)} %copy.61), kind=kOutput, calls=%fused_computation.4 | convolution fusion | flops 49104144 | bytes 10618416 | tf_op jit(solution)/shard_map/itus,itubd->itsbd/dot_general | solution.py:24
  924.3 110.7 %collective-permute-done.5 = f32[16,1,3,96,96]{4,3,2,1,0:T(8,128)} collective-permute-done((f32[16,1,3,96,96]{4,3,2,1,0:T(8,128)}, f32[16,1,3,96,96]{4,3,2,1,0:T(8,128)}, u32[]{:S(2)}, u32[]{:S(2)}) %collective-permute-start.5) | collective-permute-done | bytes 1769504 | tf_op jit(solution)/shard_map/ppermute | solution.py:9
  1035.0 14.0 %fusion.6 = f32[16,3,96,96]{2,3,1,0:T(8,128)} fusion(f32[16,1,3,96,96]{4,3,2,1,0:T(8,128)} %collective-permute-done.5, f32[16,1,3,96,96]{4,3,2,1,0:T(8,128)} %broadcast_select_fusion.1, f32[16,3,3,96,96]{4,2,3,1,0:T(4,128)S(1)} %fusion, f32[16,3]{1,0:T(8,128)S(1)} %bitcast.51, pred[]{:T(512)S(6)} %eq.56), kind=kOutput, calls=%fused_computation.11 | convolution fusion | flops 1529708544 | bytes 10617025 | tf_op jit(solution)/shard_map/itab,itsbd->isad/dot_general | solution.py:25
  1049.1 0.1 copy.86
  1049.3 35.6 %reduce-scatter.2.cloned.1.call-done = f32[2,3,96,96]{2,3,1,0:T(8,128)} async-done(((f32[16,3,96,96]{2,3,1,0:T(8,128)}), f32[2,3,96,96]{2,3,1,0:T(8,128)}) %reduce-scatter.2.cloned.1.call-update) | async-done | bytes 221200 | tf_op jit(solution)/shard_map/reduce_scatter | solution.py:71
  1085.0 1.1 select_reduce_fusion
  1086.0 0.7 fusion.25
  1086.7 1.8 copy.76
  1088.5 106.0 %psum.7 = f32[]{:T(128)} all-reduce(f32[]{:T(128)} %fusion.25), channel_id=1, replica_groups=mesh['row'=8,'col'=8,'layer'=8] {'row','col','layer'}, use_global_device_ids=true, to_apply=%region_3.5 | all-reduce | flops 1 | bytes 8 | tf_op jit(solution)/shard_map/psum | solution.py:77
  (39 shorter events, 1.7 us)
Async XLA Ops:
  7.2 42.0 %all-gather.2.cloned.1.call-start = ((), (), s32[]{:S(2)}) async-start(), calls=%async_computation.1 | async-start | bytes 2654208 | tf_op jit(solution)/shard_map/all_gather | solution.py:47
  7.9 1077.1 %reduce-scatter.2.cloned.1.call-start = ((), (), s32[]{:S(2)}) async-start(), calls=%async_computation.2 | async-start | bytes 2654208 | tf_op jit(solution)/shard_map/reduce_scatter | solution.py:71
  49.2 187.0 %collective-permute-start = (f32[16,1,3,96,96]{4,3,2,1,0:T(8,128)}, f32[16,1,3,96,96]{4,3,2,1,0:T(8,128)S(1)}, u32[]{:S(2)}, u32[]{:S(2)}) collective-permute-start(f32[16,1,3,96,96]{4,3,2,1,0:T(8,128)} %all-gather.2.cloned.1.call-done), channel_id=1, source_target_pairs={{0,448},{64,0},{128,64},{192,128},{256,192},{320,256},{384,320},{4... | collective-permute-start | bytes 5308424 | tf_op jit(solution)/shard_map/ppermute | solution.py:9
  63.8 255.1 %collective-permute-start.3 = (f32[16,1,3,96,96]{4,3,2,1,0:T(8,128)}, f32[16,1,3,96,96]{4,3,2,1,0:T(8,128)}, u32[]{:S(2)}, u32[]{:S(2)}) collective-permute-start(f32[16,1,3,96,96]{4,3,2,1,0:T(8,128)} %all-gather.2.cloned.1.call-done), channel_id=1, source_target_pairs={{0,56},{8,0},{16,8},{24,16},{32,24},{40,32},{48,40},{56,48},{1,57}... | collective-permute-start | bytes 5308424 | tf_op jit(solution)/shard_map/ppermute | solution.py:9
  236.1 1.4 copy-start.2
  324.2 4.2 copy-start.1
  324.2 191.7 %collective-permute-start.1 = (f32[16,1,3,96,96]{4,3,2,1,0:T(8,128)S(1)}, f32[16,1,3,96,96]{4,3,2,1,0:T(8,128)}, u32[]{:S(2)}, u32[]{:S(2)}) collective-permute-start(f32[16,1,3,96,96]{4,3,2,1,0:T(8,128)S(1)} %get-tuple-element.13), channel_id=1, source_target_pairs={{0,384},{64,448},{128,0},{192,64},{256,128},{320,192},{384,256},{4... | collective-permute-start | bytes 5308424 | tf_op jit(solution)/shard_map/ppermute | solution.py:9
  326.1 508.9 %collective-permute-start.4 = (f32[16,1,3,96,96]{4,3,2,1,0:T(8,128)}, f32[16,1,3,96,96]{4,3,2,1,0:T(8,128)}, u32[]{:S(2)}, u32[]{:S(2)}) collective-permute-start(f32[16,1,3,96,96]{4,3,2,1,0:T(8,128)} %get-tuple-element.14), channel_id=1, source_target_pairs={{0,48},{8,56},{16,0},{24,8},{32,16},{40,24},{48,32},{56,40},{1,49}... | collective-permute-start | bytes 5308424 | tf_op jit(solution)/shard_map/ppermute | solution.py:9
  328.4 191.6 %copy-start.4 = (s32[128,8,3]{0,1,2:T(8,128)S(1)}, s32[128,8,3]{0,1,2:T(8,128)}, u32[]{:S(2)}) copy-start(s32[128,8,3]{0,1,2:T(8,128)} %param.6) | copy-start | bytes 36868
  328.4 191.8 %copy-start.3 = (s32[128,8,3]{0,1,2:T(8,128)S(1)}, s32[128,8,3]{0,1,2:T(8,128)}, u32[]{:S(2)}) copy-start(s32[128,8,3]{0,1,2:T(8,128)} %param.7) | copy-start | bytes 36868
  517.9 320.6 %copy-start = (f32[16,1,3,96,96]{4,3,2,1,0:T(8,128)}, f32[16,1,3,96,96]{4,3,2,1,0:T(8,128)S(1)}, u32[]{:S(2)}) copy-start(f32[16,1,3,96,96]{4,3,2,1,0:T(8,128)S(1)} %broadcast_select_fusion.3) | copy-start | bytes 5308420
  517.9 375.5 %collective-permute-start.2 = (f32[16,1,3,96,96]{4,3,2,1,0:T(8,128)S(1)}, f32[16,1,3,96,96]{4,3,2,1,0:T(8,128)}, u32[]{:S(2)}, u32[]{:S(2)}) collective-permute-start(f32[16,1,3,96,96]{4,3,2,1,0:T(8,128)S(1)} %broadcast_select_fusion.3), channel_id=1, source_target_pairs={{0,256},{64,320},{128,384},{192,448},{256,0},{320,64},{384,128},{4... | collective-permute-start | bytes 5308424 | tf_op jit(solution)/shard_map/ppermute | solution.py:9
  838.5 196.6 %collective-permute-start.5 = (f32[16,1,3,96,96]{4,3,2,1,0:T(8,128)}, f32[16,1,3,96,96]{4,3,2,1,0:T(8,128)}, u32[]{:S(2)}, u32[]{:S(2)}) collective-permute-start(f32[16,1,3,96,96]{4,3,2,1,0:T(8,128)} %broadcast_select_fusion.1), channel_id=1, source_target_pairs={{0,32},{8,40},{16,48},{24,56},{32,0},{40,8},{48,16},{56,24},{1,33}... | collective-permute-start | bytes 5308424 | tf_op jit(solution)/shard_map/ppermute | solution.py:9
Sparse Core Ops, SparseCore 0:
  10.1 39.0 all-gather.1
  1049.1 35.7 reduce-scatter.1
where the time goes:
time: 1200 us
  waiting for transfers between devices  941 us (78%)
  blocking collectives  106 us (9%)
  starting transfers between devices  76.2 us (6%)
  matrix products  38.9 us (3%)
  other arithmetic  14.8 us (1%)
  between operations  14.3 us (1%)
    ppermute x6, waiting for transfers between devices, passed_along(): lax.ppermute(value, axis, [(i, (i + by) % size) for i in range(size)])  863 us
    psum x1, blocking collectives, body(): trace = lax.psum(local_trace, ('row', 'col', 'layer'))  106 us
    ppermute x6, starting transfers between devices, passed_along(): lax.ppermute(value, axis, [(i, (i + by) % size) for i in range(size)])  76.1 us
    all_gather x1, waiting for transfers between devices, body(): tile = lax.all_gather(blocks, 'layer', axis=0, tiled=True)  41.2 us
    reduce_scatter x1, waiting for transfers between devices, body(): summed = lax.psum_scatter(terms, 'layer', scatter_dimension=0, tiled=True)  35.6 us
    dot_general x1, matrix products, local_product(): jnp.einsum('itus,itubd->itsbd', match, gathered, precision=lax.Precision....  24.9 us
  transfers between devices with their start and end apart: 8, of which 7 were waited for; matrix products, arithmetic and copies ran while one was open for 3% of the time, Pallas kernels for 0%

commit v1 on v0

v1 whole, which is shorter than its diff:
```python
import functools

import jax
import jax.numpy as jnp
from jax import lax
from jax.experimental import pallas as pl
from jax.experimental.pallas import tpu as pltpu
from jax.sharding import PartitionSpec as P

MESH = pl.DeviceIdType.MESH
NX, NY, NZH, NZL, NK = 4, 4, 2, 8, 2
B, SLOTS, PACK = 96, 3, 72
HALF = SLOTS * PACK
LO = 104
NB, GROUPS, WIDTH = 128, 8, 16
MAXHIT = 2 * GROUPS * SLOTS * SLOTS


def here():
    r, c, l = lax.axis_index("row"), lax.axis_index("col"), lax.axis_index("layer")
    return {"x": r % NX, "zh": r // NX, "zl": c, "y": l // NK, "k": l % NK}


def device(at):
    return {"row": at["zh"] * NX + at["x"], "col": at["zl"], "layer": at["y"] * NK + at["k"]}


def moved(at, axis, by):
    at = dict(at)
    if axis == "x":
        at["x"] = (at["x"] + by + NX) % NX
    elif axis == "y":
        at["y"] = (at["y"] + by + NY) % NY
    elif axis == "k":
        at["k"] = 1 - at["k"]
    else:
        z = (at["zh"] * NZL + at["zl"] + by + NZH * NZL) % (NZH * NZL)
        at["zh"], at["zl"] = z // NZL, z % NZL
    return at


def pack(block):
    rest = block[PACK:, :]
    side = jnp.concatenate([rest[:, 0:32], rest[:, 32:64], rest[:, 64:96]], axis=0)
    return jnp.concatenate([block[:PACK, :], side], axis=1)


def unpack(packed):
    side = packed[:, B:]
    rest = jnp.concatenate([side[0:24], side[24:48], side[48:72]], axis=1)
    return jnp.concatenate([packed[:, :B], rest], axis=0)


def gather_kernel(b_ref, left_ref, right_ref, own, lsem, psem, csem, xsem, dsem):
    me = here()
    zl, zh, x, y, k = me["zl"], me["zh"], me["x"], me["y"], me["k"]
    partners = [moved(me, "z", 1), moved(me, "z", -1), moved(me, "z", 8), moved(me, "x", 1), moved(me, "x", -1),
                moved(me, "y", 1), moved(me, "y", -1), moved(me, "k", 1)]
    barrier = pltpu.get_barrier_semaphore()
    for other in partners:
        pl.semaphore_signal(barrier, inc=1, device_id=device(other), device_id_type=MESH)
    for i in range(2):
        for s in range(SLOTS):
            own[i, s * PACK:(s + 1) * PACK, :] = pack(b_ref[i, 0, s])
    local = [
        pltpu.make_async_copy(own, left_ref.at[zl], lsem.at[0]),
        pltpu.make_async_copy(own.at[0], right_ref.at[0, zh, k, x, y], lsem.at[1]),
        pltpu.make_async_copy(own.at[1], right_ref.at[1, zh, k, y, x], lsem.at[2]),
    ]
    for copy in local:
        copy.start()
    pl.semaphore_wait(barrier, len(partners))

    sent = []

    def send(src, dst, to, sems, index, when=None):
        copy = pltpu.make_async_remote_copy(
            src_ref=src, dst_ref=dst, send_sem=sems.at[(0,) + index], recv_sem=sems.at[(1,) + index],
            device_id=device(to), device_id_type=MESH)
        if when is None:
            copy.start()
        else:
            pl.when(when)(copy.start)
        sent.append((copy, when))
        return copy

    events = []

    far = moved(me, "z", 8)
    crossing = [
        send(own.at[0], right_ref.at[0, zh, k, x, y], far, csem, (0,)),
        send(own.at[1], right_ref.at[1, zh, k, y, x], far, csem, (1,)),
    ]

    line = {}

    def line_step(direction, n, part):
        to = moved(me, "z", direction)
        piece = jnp.clip(zl - direction * n, 0, NZL - 1)
        got = (zl >= n) if direction > 0 else (zl + n < NZL)
        more = (zl < NZL - 1) if direction > 0 else (zl > 0)
        slot = 0 if direction > 0 else 1
        if n > 0:
            pl.when(got)(line[direction, n - 1, part].wait_recv)
        if n < NZL - 1:
            src = own.at[part] if n == 0 else left_ref.at[piece, part]
            line[direction, n, part] = send(
                src, left_ref.at[piece, part], to, psem, (slot, n, part), jnp.logical_and(got, more))

    for part in range(2):
        for direction in (1, -1):
            line_step(direction, 0, part)
    for n in range(1, NZL):
        for part in range(2):
            for direction in (1, -1):
                events.append((5.0 * n + 2.5 * part, functools.partial(line_step, direction, n, part)))

    def plane(phase, half, start):
        first = ("x", "y")
        second = ("y", "x")
        size = {"x": NX, "y": NY}
        chunks = {}

        def ref(ab, p, q, rows=None):
            view = right_ref.at[ab, half, k, p, q]
            return view if rows is None else view.at[pl.ds(rows[0], rows[1])]

        lo, hi = (0, LO), (LO, HALF - LO)

        def spot(axis, by):
            return (me[axis] + by + size[axis]) % size[axis]

        def spread(ab, j):
            a, b = first[ab], second[ab]
            p, q = spot(a, j), me[b]
            for d, way in enumerate((1, -1)):
                chunks[ab, "b", j, d] = send(ref(ab, p, q), ref(ab, p, q), moved(me, b, way), xsem, (phase, ab, 4 + 4 * j + d))

        def begin(ab):
            a = first[ab]
            p, q = me[a], me[second[ab]]
            if phase == 1:
                crossing[ab].wait_recv()
            for d, way in enumerate((1, -1)):
                chunks[ab, "a", d] = send(ref(ab, p, q), ref(ab, p, q), moved(me, a, way), xsem, (phase, ab, d))
            spread(ab, 0)

        def pass_on(ab, d):
            way = 1 - 2 * d
            a = first[ab]
            p, q = spot(a, -way), me[second[ab]]
            chunks[ab, "a", d].wait_recv()
            rows = lo if d == 0 else hi
            chunks[ab, "a2", d] = send(ref(ab, p, q, rows), ref(ab, p, q, rows), moved(me, a, way), xsem, (phase, ab, 2 + d))
            spread(ab, 3 if way > 0 else 1)

        def opposite(ab):
            for d in range(2):
                chunks[ab, "a2", d].wait_recv()
            spread(ab, 2)

        def pass_second(ab, j):
            a, b = first[ab], second[ab]
            p = spot(a, j)
            for d, way in enumerate((1, -1)):
                q = spot(b, -way)
                chunks[ab, "b", j, d].wait_recv()
                rows = lo if d == 0 else hi
                chunks[ab, "b2", j, d] = send(ref(ab, p, q, rows), ref(ab, p, q, rows), moved(me, b, way), xsem, (phase, ab, 6 + 4 * j + d))

        def share(ab, j):
            for d in range(2):
                chunks[ab, "b2", j, d].wait_recv()
            p = spot(first[ab], j)
            src = right_ref.at[ab, half, k, p]
            chunks[ab, "c", j] = send(src, src, moved(me, "k", 1), dsem, (phase, ab, j))

        def finish(ab, j):
            chunks[ab, "c", j].wait_recv()

        order = [(0.0, begin)]
        for d in range(2):
            order.append((2.5, lambda ab, d=d: pass_on(ab, d)))
        order.append((6.0, lambda ab: pass_second(ab, 0)))
        order.append((7.0, lambda ab: opposite(ab)))
        order.append((10.0, lambda ab: pass_second(ab, 3)))
        order.append((11.0, lambda ab: share(ab, 0)))
        order.append((12.0, lambda ab: pass_second(ab, 1)))
        order.append((15.0, lambda ab: share(ab, 3)))
        order.append((15.0, lambda ab: pass_second(ab, 2)))
        order.append((16.0, lambda ab: share(ab, 1)))
        order.append((19.0, lambda ab: share(ab, 2)))
        for j in range(4):
            order.append((100.0, lambda ab, j=j: finish(ab, j)))
        for at, step in order:
            for ab in range(2):
                events.append((start + at, functools.partial(step, ab)))

    for copy in local:
        copy.wait()
    plane(0, zh, 0.0)
    plane(1, 1 - zh, 20.0)
    for _, step in sorted(events, key=lambda e: e[0]):
        step()
    for copy, when in sent:
        if when is None:
            copy.wait_send()
        else:
            pl.when(when)(copy.wait_send)


def gather(blocks):
    return pl.pallas_call(
        gather_kernel,
        out_shape=(
            jax.ShapeDtypeStruct((NZL, 2, HALF, 128), jnp.float32),
            jax.ShapeDtypeStruct((2, NZH, NK, 4, 4, HALF, 128), jnp.float32),
        ),
        in_specs=[pl.BlockSpec(memory_space=pltpu.VMEM)],
        out_specs=(pl.BlockSpec(memory_space=pltpu.HBM), pl.BlockSpec(memory_space=pltpu.HBM)),
        scratch_shapes=[
            pltpu.VMEM((2, HALF, 128), jnp.float32),
            pltpu.SemaphoreType.DMA((3,)),
            pltpu.SemaphoreType.DMA((2, 2, NZL - 1, 2)),
            pltpu.SemaphoreType.DMA((2, 2)),
            pltpu.SemaphoreType.DMA((2, 2, 2, 20)),
            pltpu.SemaphoreType.DMA((2, 2, 2, 4)),
        ],
        compiler_params=pltpu.CompilerParams(collective_id=0, has_side_effects=True, vmem_limit_bytes=16 << 20),
        name="gather_rows_and_columns",
    )(blocks)


def product_kernel(table, left_ref, right_ref, out_ref, part_ref, held, codes, sem):
    me = here()
    c = me["zl"]
    row = lax.axis_index("row")
    first = row * WIDTH + lax.axis_index("layer") * 2
    out_ref[...] = jnp.zeros_like(out_ref)

    def fetch(n, code):
        m = code // 16
        u = code // 4 % 4
        group, inner = m // WIDTH, m % WIDTH
        ab, ky, kk = inner % 2, inner // 4, inner // 2 % 2
        gx = group % NX
        p = jnp.where(ab == 0, gx, ky)
        q = jnp.where(ab == 0, ky, gx)
        return pltpu.make_async_copy(
            right_ref.at[ab, group // NX, kk, p, q, pl.ds(pl.multiple_of(u * PACK, 8), PACK)], held.at[n], sem.at[n])

    def find(e, n):
        i, slot = e // (GROUPS * SLOTS), e % (GROUPS * SLOTS)
        at = first + i
        base = at * (GROUPS * SLOTS)
        col = table[base + slot]
        m = slot // SLOTS * WIDTH + col

        def inner(n):
            for u in range(SLOTS):
                j = table[m * (GROUPS * SLOTS) + c * SLOTS + u]
                s = jnp.int32(3)
                for t in range(SLOTS):
                    s = jnp.where(j == table[base + c * SLOTS + t], t, s)
                hit = jnp.logical_and(j >= 0, s < 3)
                code = (m * 4 + u) * 4 + s

                @pl.when(hit)
                def _():
                    codes[2 * n] = code
                    codes[2 * n + 1] = e
                    fetch(n, code).start()

                n = n + hit.astype(jnp.int32)
            return n

        return lax.cond(col >= 0, inner, lambda n: n, n)

    count = lax.fori_loop(0, 2 * GROUPS * SLOTS, find, jnp.int32(0))

    def multiply(n, _):
        code, e = codes[2 * n], codes[2 * n + 1]
        i, slot = e // (GROUPS * SLOTS), e % (GROUPS * SLOTS)
        fetch(n, code).wait()
        start = pl.multiple_of(slot % SLOTS * PACK, 8)
        a = unpack(left_ref[slot // SLOTS, i, pl.ds(start, PACK), :])
        b = unpack(held[n])
        a_hi, b_hi = a.astype(jnp.bfloat16), b.astype(jnp.bfloat16)
        a_lo = (a - a_hi.astype(jnp.float32)).astype(jnp.bfloat16)
        b_lo = (b - b_hi.astype(jnp.float32)).astype(jnp.bfloat16)
        dot = functools.partial(jnp.dot, preferred_element_type=jnp.float32)
        out_ref[i, 0, code % 4] += dot(a_hi, b_hi) + (dot(a_lo, b_hi) + dot(a_hi, b_lo))
        return 0

    lax.fori_loop(0, count, multiply, 0)

    part_ref[...] = jnp.zeros_like(part_ref)

    @pl.when(row == c)
    def _():
        total = jnp.float32(0)
        eye = lax.broadcasted_iota(jnp.int32, (B, B), 0) == lax.broadcasted_iota(jnp.int32, (B, B), 1)
        for i in range(2):
            for s in range(SLOTS):
                on = table[(first + i) * (GROUPS * SLOTS) + c * SLOTS + s] == (first + i) % WIDTH
                total += jnp.sum(jnp.where(jnp.logical_and(eye, on), out_ref[i, 0, s], 0.0))
        part_ref[...] = jnp.full(part_ref.shape, total, jnp.float32)


def local_product(table, left, right):
    return pl.pallas_call(
        product_kernel,
        out_shape=(
            jax.ShapeDtypeStruct((2, 1, SLOTS, B, B), jnp.float32),
            jax.ShapeDtypeStruct((8, 128), jnp.float32),
        ),
        in_specs=[
            pl.BlockSpec(memory_space=pltpu.SMEM),
            pl.BlockSpec(memory_space=pltpu.VMEM),
            pl.BlockSpec(memory_space=pltpu.HBM),
        ],
        out_specs=(pl.BlockSpec(memory_space=pltpu.VMEM), pl.BlockSpec(memory_space=pltpu.VMEM)),
        scratch_shapes=[
            pltpu.VMEM((MAXHIT, PACK, 128), jnp.float32),
            pltpu.SMEM((2 * MAXHIT,), jnp.int32),
            pltpu.SemaphoreType.DMA((MAXHIT,)),
        ],
        compiler_params=pltpu.CompilerParams(vmem_limit_bytes=24 << 20),
        name="matched_products",
    )(table, left, right)


def total_kernel(v_ref, o_ref, in_plane, along, one, psem, zsem):
    me = here()
    z = me["zh"] * NZL + me["zl"]
    mine = (me["x"] * NY + me["y"]) * NK + me["k"]
    n_plane, n_z = NX * NY * NK, NZH * NZL
    barrier = pltpu.get_barrier_semaphore()

    def in_plane_at(j):
        t = (mine + j) % n_plane
        return {"x": t // (NY * NK), "y": t // NK % NY, "k": t % NK, "zh": me["zh"], "zl": me["zl"]}

    for j in range(1, n_plane):
        pl.semaphore_signal(barrier, inc=1, device_id=device(in_plane_at(j)), device_id_type=MESH)
    for j in range(1, n_z):
        pl.semaphore_signal(barrier, inc=1, device_id=device(moved(me, "z", j)), device_id_type=MESH)
    in_plane[mine] = v_ref[...]
    pl.semaphore_wait(barrier, n_plane + n_z - 2)
    copies = []
    for j in range(1, n_plane):
        copy = pltpu.make_async_remote_copy(
            src_ref=in_plane.at[mine], dst_ref=in_plane.at[mine], send_sem=psem.at[0, j], recv_sem=psem.at[1, j],
            device_id=device(in_plane_at(j)), device_id_type=MESH)
        copy.start()
        copies.append(copy)
    for copy in copies:
        copy.wait_recv()
    one[...] = jnp.sum(in_plane[...], axis=0)
    along[z] = one[...]
    more = []
    for j in range(1, n_z):
        copy = pltpu.make_async_remote_copy(
            src_ref=one, dst_ref=along.at[z], send_sem=zsem.at[0, j], recv_sem=zsem.at[1, j],
            device_id=device(moved(me, "z", j)), device_id_type=MESH)
        copy.start()
        more.append(copy)
    for copy in more:
        copy.wait_recv()
    o_ref[...] = jnp.sum(along[...], axis=0)
    for copy in copies + more:
        copy.wait_send()


def total(part):
    return pl.pallas_call(
        total_kernel,
        out_shape=jax.ShapeDtypeStruct((8, 128), jnp.float32),
        in_specs=[pl.BlockSpec(memory_space=pltpu.VMEM)],
        out_specs=pl.BlockSpec(memory_space=pltpu.VMEM),
        scratch_shapes=[
            pltpu.VMEM((NX * NY * NK, 8, 128), jnp.float32),
            pltpu.VMEM((NZH * NZL, 8, 128), jnp.float32),
            pltpu.VMEM((8, 128), jnp.float32),
            pltpu.SemaphoreType.DMA((2, NX * NY * NK)),
            pltpu.SemaphoreType.DMA((2, NZH * NZL)),
        ],
        compiler_params=pltpu.CompilerParams(collective_id=1, has_side_effects=True),
        name="trace_total",
    )(part)


def body(blocks, block_cols, occupancy):
    table = jnp.where(occupancy == 1, block_cols, -1).reshape(-1)
    left, right = gather(blocks)
    product, part = local_product(table, left, right)
    return product, total(part)[0, 0]


def solution(mesh):
    in_specs = (P(("row", "layer"), "col", None, None, None), P(), P())
    out_specs = (P(("row", "layer"), "col", None, None, None), P())
    return jax.shard_map(body, mesh=mesh, in_specs=in_specs, out_specs=out_specs, check_vma=False)
```

time: 1200 us -> 121 us (0.10)
  waiting for transfers between devices: 941 us -> 0 us
  Pallas kernels: 0 us -> 116 us
  blocking collectives: 106 us -> 0 us
  starting transfers between devices: 76.2 us -> 0 us
  matrix products: 38.9 us -> 0 us
  other arithmetic: 14.8 us -> 0.73 us
  between operations: 14.3 us -> 0.68 us
    ppermute x6 -> x0, waiting for transfers between devices: 863 us -> none  [passed_along(): lax.ppermute(value, axis, [(i, (i + by) % size) for i in range(size)])]
    pallas_call x0 -> x3, Pallas kernels: none -> 116 us  [the longest x1 83.3 us: gather(): pl.pallas_call(gather_kernel, out_shape=(jax.ShapeDtypeStruct((NZL, 2, HA...]
    psum x1 -> x0, blocking collectives: 106 us -> none  [body(): trace = lax.psum(local_trace, ('row', 'col', 'layer'))]
    ppermute x6 -> x0, starting transfers between devices: 76.1 us -> none  [passed_along(): lax.ppermute(value, axis, [(i, (i + by) % size) for i in range(size)])]
    all_gather x1 -> x0, waiting for transfers between devices: 41.2 us -> none  [body(): tile = lax.all_gather(blocks, 'layer', axis=0, tiled=True)]
    dot_general x2 -> x0, matrix products: 38.9 us -> none  [the longest x1 24.9 us: local_product(): jnp.einsum('itus,itubd->itsbd', match, gathered, precision=lax.Precision....]
    reduce_scatter x1 -> x0, waiting for transfers between devices: 35.6 us -> none  [body(): summed = lax.psum_scatter(terms, 'layer', scatter_dimension=0, tiled=True)]
  transfers between devices with their start and end apart: 8 -> 0, of which waited for: 7 -> 0; matrix products, arithmetic and copies ran while one was open for 3% -> 0% of each run, Pallas kernels for 0% -> 0%
where the time goes in v1:
time: 121 us
  Pallas kernels  116 us (96%)
  local copies, waits for them, and re-layouts  3.27 us (3%)
    pallas_call x1, Pallas kernels, gather(): pl.pallas_call(gather_kernel, out_shape=(jax.ShapeDtypeStruct((NZL, 2, HA...  83.3 us
    pallas_call x1, Pallas kernels, total(): pl.pallas_call(total_kernel, out_shape=jax.ShapeDtypeStruct((8, 128), jnp...  24 us
    pallas_call x1, Pallas kernels, local_product(): pl.pallas_call(product_kernel, out_shape=(jax.ShapeDtypeStruct((2, 1, SLO...  9.03 us

profile of v1, /device:TPU:1, one launch (start us, length us, event | category | flops | bytes accessed | tf_op | source)
XLA Modules:
  0.0 121.0 jit_solution(11397025637041652274)
XLA Ops:
  0.6 0.7 compare_select_fusion
  1.4 0.3 copy.5
  1.6 0.3 reshape.7.table
  1.9 0.0 copy-start
  1.9 1.0 copy-done
  2.9 83.3 %gather_rows_and_columns.1 = (f32[8,2,216,128]{3,2,1,0:T(8,128)S(1)}, f32[2,2,2,4,4,216,128]{6,5,4,3,2,1,0:T(8,128)S(1)}) custom-call(f32[2,1,3,96,96]{4,3,2,1,0:T(8,128)S(1)} %copy-done), custom_call_target="tpu_custom_call" | custom-call | tf_op jit(solution)/shard_map/gather_rows_and_columns/pallas_call | solution.py:213
  86.2 9.0 %matched_products.1 = (f32[2,1,3,96,96]{4,3,2,1,0:T(8,128)}, f32[8,128]{1,0:T(8,128)S(1)}) custom-call(s32[3072]{0:T(1024)S(1)} %reshape.7.table, f32[8,2,216,128]{3,2,1,0:T(8,128)S(1)} %get-tuple-element.6.left_ref, f32[2,2,2,4,4,216,128]{6,5,4,3,2,1,0:T(8,128)S(1)} %get-tuple-element.7.right_ref), custom_call_target="tpu_custom_call" | custom-call | tf_op jit(solution)/shard_map/matched_products/pallas_call | solution.py:311
  95.2 0.0 copy-start.1
  95.3 0.6 copy-done.1
  95.8 24.0 %trace_total.1 = f32[8,128]{1,0:T(8,128)} custom-call(f32[8,128]{1,0:T(8,128)} %copy-done.1), custom_call_target="tpu_custom_call" | custom-call | tf_op jit(solution)/shard_map/trace_total/pallas_call | solution.py:376
  119.8 1.2 slice.3
Async XLA Ops:
  1.9 1.0 copy-start
  95.2 0.6 copy-start.1

commit v2 on v0

v2 whole, which is shorter than its diff:
```python
import functools

import jax
import jax.numpy as jnp
from jax import lax
from jax.experimental import pallas as pl
from jax.experimental.pallas import tpu as pltpu
from jax.sharding import PartitionSpec as P

MESH = pl.DeviceIdType.MESH
NX, NY, NZH, NZL, NK = 4, 4, 2, 8, 2
NZ = NZH * NZL
B, SLOTS, PACK = 96, 3, 72
CUT = 32
NB, GROUPS, WIDTH = 128, 8, 16
ROW = GROUPS * SLOTS
QUAD = GROUPS // NZH
DEPTH = QUAD * SLOTS * 128

T_RING, T_TAIL0, T_TAIL, T_FAR = 2.7, 12.0, 3.0, 21.6
AT_NEAR, AT_LEFT = 29.6, 36.0


def here():
    r, c, l = lax.axis_index("row"), lax.axis_index("col"), lax.axis_index("layer")
    return {"x": r % NX, "zh": r // NX, "zl": c, "y": l // NK, "k": l % NK}


def device(at):
    return {"row": at["zh"] * NX + at["x"], "col": at["zl"], "layer": at["y"] * NK + at["k"]}


def moved(at, axis, by):
    at = dict(at)
    if axis == "x":
        at["x"] = (at["x"] + by + NX) % NX
    elif axis == "y":
        at["y"] = (at["y"] + by + NY) % NY
    elif axis == "k":
        at["k"] = 1 - at["k"]
    else:
        z = (at["zh"] * NZL + at["zl"] + by + NZ) % NZ
        at["zh"], at["zl"] = z // NZL, z % NZL
    return at


def pack(block):
    rest = block[PACK:, :]
    side = jnp.concatenate([rest[:, 0:32], rest[:, 32:64], rest[:, 64:96]], axis=0)
    return jnp.concatenate([block[:PACK, :], side], axis=1)


def unpack(packed):
    side = packed[:, B:]
    rest = jnp.concatenate([side[0:24], side[24:48], side[48:72]], axis=1)
    return jnp.concatenate([packed[:, :B], rest], axis=0)


def split(value):
    high = value.astype(jnp.bfloat16)
    return high, (value - high.astype(jnp.float32)).astype(jnp.bfloat16)


def kernel(table, b_ref, out_ref, trace_ref, raw, own, line, near, far, lhs, rhs_hi, rhs_lo, in_plane, along, one, two,
           lsem, s1sem, s2sem, xsem, dsem, psem, zsem):
    me = here()
    zl, zh, x, y, k = me["zl"], me["zh"], me["x"], me["y"], me["k"]
    z = zh * NZL + zl
    partners = [moved(me, *step) for step in (
        ("z", 1), ("z", -1), ("x", 1), ("x", -1), ("x", 2), ("y", 1), ("y", -1), ("y", 2), ("k", 1))]
    barrier = pltpu.get_barrier_semaphore()
    for other in partners:
        pl.semaphore_signal(barrier, inc=1, device_id=device(other), device_id_type=MESH)
    load = pltpu.make_async_copy(b_ref, raw, lsem.at[0])
    load.start()
    load.wait()
    for i in range(2):
        for s in range(SLOTS):
            own[i, s] = pack(raw[i, 0, s])
    local = [
        pltpu.make_async_copy(own, line.at[z], lsem.at[0]),
        pltpu.make_async_copy(own.at[0], near.at[0, k, x, y], lsem.at[1]),
        pltpu.make_async_copy(own.at[1], near.at[1, k, x, y], lsem.at[2]),
    ]
    for copy in local:
        copy.start()
    pl.semaphore_wait(barrier, len(partners))

    sent = []

    def send(src, dst, to, sems, index, when=None):
        copy = pltpu.make_async_remote_copy(
            src_ref=src, dst_ref=dst, send_sem=sems.at[(0,) + index], recv_sem=sems.at[(1,) + index],
            device_id=device(to), device_id_type=MESH)
        if when is None:
            copy.start()
        else:
            pl.when(when)(copy.start)
        sent.append((copy, when))
        return copy

    events = []

    ring, tail = {}, {}

    def ring_step(d, n, c):
        way = 1 - 2 * d
        origin = (z - way * n + NZ) % NZ
        if n > 0:
            ring[d, n - 1, c].wait_recv()
        if n < NZL:
            src = own.at[d, c] if n == 0 else line.at[origin, d, c]
            dst = line.at[origin, d, c] if n < NZL - 1 else far.at[d, k, x, y, c]
            ring[d, n, c] = send(src, dst, moved(me, "z", way), s1sem, (d, n, c))

    def tail_step(d, n, c):
        way = 1 - 2 * d
        part = 1 - d
        piece = jnp.clip(zl - way * n, 0, NZL - 1)
        origin = zh * NZL + piece
        got = (zl >= n) if d == 0 else (zl + n < NZL)
        more = (zl < NZL - 1) if d == 0 else (zl > 0)
        if n > 0:
            pl.when(got)(tail[d, n - 1, c].wait_recv)
        if n < NZL - 1:
            src = own.at[part, c] if n == 0 else line.at[origin, part, c]
            tail[d, n, c] = send(src, line.at[origin, part, c], moved(me, "z", way), s2sem, (d, n, c),
                                 jnp.logical_and(got, more))

    for n in range(NZL):
        for c in range(SLOTS):
            for d in range(2):
                events.append((T_RING * n + 0.76 * c, functools.partial(ring_step, d, n, c)))
                events.append((2.3 if n == 0 else T_TAIL0 + T_TAIL * n + 0.76 * c, functools.partial(tail_step, d, n, c)))

    def plane(phase, store, start):
        first, second = ("x", "y"), ("y", "x")
        size = {"x": NX, "y": NY}
        chunks = {}

        def ref(ab, p, q, d=None):
            view = store.at[ab, k, p, q] if ab == 0 else store.at[ab, k, q, p]
            if d is None:
                return view
            low = CUT if ab == 0 else PACK - CUT
            return view.at[:, pl.ds(0, low)] if d == 0 else view.at[:, pl.ds(low, PACK - low)]

        def spot(axis, by):
            return (me[axis] + by + size[axis]) % size[axis]

        def go(ab, p, q, axis, way, sem, d=None):
            r = ref(ab, p, q, d)
            return send(r, r, moved(me, axis, way), xsem, (phase, ab, sem))

        def spread(ab, j):
            a, b = first[ab], second[ab]
            for d, way in enumerate((1, -1)):
                chunks[ab, "b", j, d] = go(ab, spot(a, j), me[b], b, way, 3 + 4 * j + d)

        def begin(ab):
            a = first[ab]
            if phase == 1:
                for c in range(SLOTS):
                    ring_step(ab, NZL, c)
            for d, way in enumerate((1, -1, 2)):
                chunks[ab, "a", d] = go(ab, me[a], me[second[ab]], a, way, d)

        def pass_on(ab, d):
            chunks[ab, "a", d].wait_recv()
            spread(ab, (3, 1, 2)[d])

        def pass_second(ab, j):
            a, b = first[ab], second[ab]
            for d, way in enumerate((1, -1)):
                chunks[ab, "b", j, d].wait_recv()
                chunks[ab, "b2", j, d] = go(ab, spot(a, j), spot(b, -way), b, way, 5 + 4 * j + d, d)

        def share(ab, j):
            for d in range(2):
                chunks[ab, "b2", j, d].wait_recv()
            p = spot(first[ab], j)
            src = store.at[ab, k, p] if ab == 0 else store.at[ab, k, :, p]
            chunks[ab, "c", j] = send(src, src, moved(me, "k", 1), dsem, (phase, ab, j))

        def finish(ab, j):
            chunks[ab, "c", j].wait_recv()

        order = [
            (0.0, begin), (0.01, lambda ab: spread(ab, 0)),
            (4.5, lambda ab: pass_on(ab, 0)), (4.5, lambda ab: pass_on(ab, 1)),
            (9.0, lambda ab: pass_on(ab, 2)), (9.1, lambda ab: pass_second(ab, 0)),
            (12.5, lambda ab: pass_second(ab, 3)), (14.7, lambda ab: pass_second(ab, 1)),
            (15.8, lambda ab: share(ab, 0)), (18.1, lambda ab: share(ab, 3)),
            (18.2, lambda ab: pass_second(ab, 2)), (20.4, lambda ab: share(ab, 1)), (22.6, lambda ab: share(ab, 2)),
        ]
        for j in range(4):
            order.append((24.0 if phase == 0 else 1000.0, lambda ab, j=j: finish(ab, j)))
        for at, step in order:
            for ab in range(2):
                events.append((start + at, functools.partial(step, ab)))

    for copy in local:
        copy.wait()
    plane(0, near, 0.0)
    plane(1, far, T_FAR)

    first_row = lax.axis_index("row") * WIDTH + lax.axis_index("layer") * 2

    def left_side(i, half, h, g4):
        for t in range(SLOTS):
            high, low = split(unpack(line[zh * NZL + h * QUAD + g4, i, t]))
            lanes = pl.ds(pl.multiple_of((g4 * SLOTS + t) * 128, 128), B)
            lhs[i, half, 0:B, lanes] = high
            lhs[i, half, B:2 * B, lanes] = low

    def right_side(i, half, h, g4):
        store = near if half == 0 else far
        base = (first_row + i) * ROW
        group = h * QUAD + g4
        wanted = [table[base + zl * SLOTS + s] for s in range(SLOTS)]
        for t in range(SLOTS):
            col = table[base + group * SLOTS + t]
            inner = jnp.maximum(col, 0)
            at = (group * WIDTH + inner) * ROW + zl * SLOTS
            cols = [table[at + u] for u in range(SLOTS)]
            depth = pl.ds(pl.multiple_of((g4 * SLOTS + t) * 128, 128), B)
            for s in range(SLOTS):
                want = jnp.where(col >= 0, wanted[s] + 1, 0)
                hits = [jnp.where(cols[u] + 1 == want, 1, 0) * jnp.where(want > 0, 1, 0) for u in range(SLOTS)]
                u = jnp.minimum(hits[1] + 2 * hits[2], SLOTS - 1)
                on = jnp.minimum(hits[0] + hits[1] + hits[2], 1).astype(jnp.float32)
                block = store[inner & 1, (inner >> 1) & 1, g4, inner >> 2, u] * on
                high, low = split(unpack(block))
                rhs_hi[i, half, depth, s * 128:s * 128 + B] = high
                rhs_lo[i, half, depth, s * 128:s * 128 + B] = low

    def multiply(i, half):
        dot = functools.partial(jnp.dot, preferred_element_type=jnp.float32)
        main = dot(lhs[i, half], rhs_hi[i, half])
        rest = dot(lhs[i, half, 0:B, :], rhs_lo[i, half])
        value = main[0:B] + (main[B:] + rest)
        for s in range(SLOTS):
            part = value[:, s * 128:s * 128 + B]
            if half == 0:
                out_ref[i, 0, s] = part
            else:
                out_ref[i, 0, s] += part

    def clear(ref):
        ref[...] = jnp.zeros_like(ref)

    def prepare():
        for i in range(2):
            for half in range(2):
                clear(lhs.at[i, half])
                clear(rhs_hi.at[i, half])
                clear(rhs_lo.at[i, half])

    def every(fn, half, h):
        def step(n, _):
            fn(n // QUAD, half, h, n % QUAD)
            return 0
        lax.fori_loop(0, 2 * QUAD, step, 0)

    other = 1 - zh
    events.append((0.3, prepare))
    events.append((AT_NEAR, lambda: every(right_side, 0, zh)))
    events.append((AT_LEFT, lambda: every(left_side, 0, zh)))
    events.append((AT_LEFT + 1.5, lambda: every(left_side, 1, other)))
    for i in range(2):
        events.append((AT_LEFT + 2.5 + i, functools.partial(multiply, i, 0)))
    for _, step in sorted(events, key=lambda e: e[0]):
        step()
    every(right_side, 1, other)
    for i in range(2):
        multiply(i, 1)

    row, col = lax.axis_index("row"), lax.axis_index("col")
    diagonal = row == col
    n_yk = NY * NK
    def own_trace():
        eye = lax.broadcasted_iota(jnp.int32, (B, B), 0) == lax.broadcasted_iota(jnp.int32, (B, B), 1)
        total = jnp.zeros((1, B), jnp.float32)
        for i in range(2):
            for s in range(SLOTS):
                at = first_row + i
                on = table[at * ROW + zl * SLOTS + s] == at % WIDTH
                total += jnp.sum(jnp.where(eye, out_ref[i, 0, s], 0.0), axis=0, keepdims=True) * jnp.where(on, 1.0, 0.0)
        one[...] = jnp.full((8, 128), jnp.sum(total), jnp.float32)

    mine = y * NK + k

    def plane_copy(j):
        dx, t = (2, 1, 3, 0)[j // n_yk], (mine + j % n_yk) % n_yk
        to = {"x": (x + dx) % NX, "y": t // NK, "k": t % NK, "zh": zh, "zl": zl}
        return pltpu.make_async_remote_copy(
            src_ref=one, dst_ref=in_plane.at[mine], send_sem=psem.at[0, j], recv_sem=psem.at[1, j],
            device_id=device(to), device_id_type=MESH)

    n_plane = NX * n_yk
    plane_copies = [plane_copy(j) for j in range(n_plane) if j != 3 * n_yk]

    @pl.when(diagonal)
    def _():
        own_trace()
        for copy in plane_copies:
            copy.start()
        in_plane[mine] = one[...]

    holds = zh == zl // NX
    dx_in = (x - zl % NX + NX) % NX
    for slot, dx in enumerate((2, 1, 3, 0)):
        @pl.when(jnp.logical_and(holds, dx_in == dx))
        def _():
            for t in range(n_yk):
                if dx != 0 or t != 0:
                    plane_copy(slot * n_yk + t).wait_recv()

    def z_copy(j):
        return pltpu.make_async_remote_copy(
            src_ref=two, dst_ref=along.at[zl], send_sem=zsem.at[0, j], recv_sem=zsem.at[1, j],
            device_id=device(moved(me, "z", j)), device_id_type=MESH)

    z_order = sorted(range(1, NZ), key=lambda j: -min(j, NZ - j))

    @pl.when(holds)
    def _():
        two[...] = jnp.sum(in_plane[...], axis=0)
        for j in z_order:
            z_copy(j).start()
        along[zl] = two[...]

    for j in range(1, NZ):
        zs = (z - j + NZ) % NZ
        @pl.when(zs // NZL == zs % NZL // NX)
        def _():
            z_copy(j).wait_recv()
    trace_ref[...] = jnp.sum(along[...], axis=0)

    @pl.when(holds)
    def _():
        for j in z_order:
            z_copy(j).wait_send()

    @pl.when(diagonal)
    def _():
        for copy in plane_copies:
            copy.wait_send()
    for copy, when in sent:
        if when is None:
            copy.wait_send()
        else:
            pl.when(when)(copy.wait_send)


def square(table, blocks, collective_id=0, name="square"):
    return pl.pallas_call(
        kernel,
        out_shape=(jax.ShapeDtypeStruct((2, 1, SLOTS, B, B), jnp.float32), jax.ShapeDtypeStruct((8, 128), jnp.float32)),
        in_specs=[pl.BlockSpec(memory_space=pltpu.SMEM), pl.BlockSpec(memory_space=pl.ANY)],
        out_specs=(pl.BlockSpec(memory_space=pltpu.VMEM), pl.BlockSpec(memory_space=pltpu.VMEM)),
        scratch_shapes=[
            pltpu.VMEM((2, 1, SLOTS, B, B), jnp.float32),
            pltpu.VMEM((2, SLOTS, PACK, 128), jnp.float32),
            pltpu.VMEM((NZ, 2, SLOTS, PACK, 128), jnp.float32),
            pltpu.VMEM((2, NK, NX, NY, SLOTS, PACK, 128), jnp.float32),
            pltpu.VMEM((2, NK, NX, NY, SLOTS, PACK, 128), jnp.float32),
            pltpu.VMEM((2, 2, 2 * B, DEPTH), jnp.bfloat16),
            pltpu.VMEM((2, 2, DEPTH, SLOTS * 128), jnp.bfloat16),
            pltpu.VMEM((2, 2, DEPTH, SLOTS * 128), jnp.bfloat16),
            pltpu.VMEM((NY * NK, 8, 128), jnp.float32),
            pltpu.VMEM((NZL, 8, 128), jnp.float32),
            pltpu.VMEM((8, 128), jnp.float32),
            pltpu.VMEM((8, 128), jnp.float32),
            pltpu.SemaphoreType.DMA((3,)),
            pltpu.SemaphoreType.DMA((2, 2, NZL, SLOTS)),
            pltpu.SemaphoreType.DMA((2, 2, NZL, SLOTS)),
            pltpu.SemaphoreType.DMA((2, 2, 2, 20)),
            pltpu.SemaphoreType.DMA((2, 2, 2, 4)),
            pltpu.SemaphoreType.DMA((2, NX * NY * NK)),
            pltpu.SemaphoreType.DMA((2, NZ)),
        ],
        compiler_params=pltpu.CompilerParams(collective_id=collective_id, has_side_effects=True, vmem_limit_bytes=48 << 20),
        name=name,
    )(table, blocks)


def body(blocks, block_cols, occupancy):
    table = jnp.where(occupancy == 1, block_cols, -1).reshape(-1)
    product, trace = square(table, blocks)
    return product, trace[0, 0]


def solution(mesh):
    in_specs = (P(("row", "layer"), "col", None, None, None), P(), P())
    out_specs = (P(("row", "layer"), "col", None, None, None), P())
    return jax.shard_map(body, mesh=mesh, in_specs=in_specs, out_specs=out_specs, check_vma=False)
```

time: 1200 us -> 90.5 us (0.08)
  waiting for transfers between devices: 941 us -> 0 us
  blocking collectives: 106 us -> 0 us
  Pallas kernels: 0 us -> 86.4 us
  starting transfers between devices: 76.2 us -> 0 us
  matrix products: 38.9 us -> 0 us
  other arithmetic: 14.8 us -> 0.73 us
  between operations: 14.3 us -> 0.65 us
    ppermute x6 -> x0, waiting for transfers between devices: 863 us -> none  [passed_along(): lax.ppermute(value, axis, [(i, (i + by) % size) for i in range(size)])]
    psum x1 -> x0, blocking collectives: 106 us -> none  [body(): trace = lax.psum(local_trace, ('row', 'col', 'layer'))]
    pallas_call x0 -> x1, Pallas kernels: none -> 86.4 us  [square(): pl.pallas_call(kernel, out_shape=(jax.ShapeDtypeStruct((2, 1, SLOTS, B, B...]
    ppermute x6 -> x0, starting transfers between devices: 76.1 us -> none  [passed_along(): lax.ppermute(value, axis, [(i, (i + by) % size) for i in range(size)])]
    all_gather x1 -> x0, waiting for transfers between devices: 41.2 us -> none  [body(): tile = lax.all_gather(blocks, 'layer', axis=0, tiled=True)]
    dot_general x2 -> x0, matrix products: 38.9 us -> none  [the longest x1 24.9 us: local_product(): jnp.einsum('itus,itubd->itsbd', match, gathered, precision=lax.Precision....]
    reduce_scatter x1 -> x0, waiting for transfers between devices: 35.6 us -> none  [body(): summed = lax.psum_scatter(terms, 'layer', scatter_dimension=0, tiled=True)]
  transfers between devices with their start and end apart: 8 -> 0, of which waited for: 7 -> 0; matrix products, arithmetic and copies ran while one was open for 3% -> 0% of each run, Pallas kernels for 0% -> 0%
where the time goes in v2:
time: 90.5 us; the launch traced here: 90.2 us
  Pallas kernels  86.4 us (95%)
  local copies, waits for them, and re-layouts  2.44 us (3%)
    pallas_call x1, Pallas kernels, square(): pl.pallas_call(kernel, out_shape=(jax.ShapeDtypeStruct((2, 1, SLOTS, B, B...  86.4 us

profile of v2, /device:TPU:1, one launch (start us, length us, event | category | flops | bytes accessed | tf_op | source)
XLA Modules:
  0.0 90.2 jit_solution(7731062808568597286)
XLA Ops:
  0.6 0.7 compare_select_fusion
  1.4 0.3 copy.5
  1.6 0.0 copy-start
  1.6 0.3 reshape.7.table
  1.9 0.7 copy-done
  2.6 86.4 %square.1 = (f32[2,1,3,96,96]{4,3,2,1,0:T(8,128)S(1)}, f32[8,128]{1,0:T(8,128)S(1)}) custom-call(s32[3072]{0:T(1024)S(1)} %reshape.7.table, f32[2,1,3,96,96]{4,3,2,1,0:T(8,128)S(1)} %copy-done), custom_call_target="tpu_custom_call" | custom-call | tf_op jit(solution)/shard_map/square/pallas_call | solution.py:357
  89.0 0.5 slice.3
  89.5 0.7 copy.7
Async XLA Ops:
  1.6 1.0 %copy-start = (f32[2,1,3,96,96]{4,3,2,1,0:T(8,128)S(1)}, f32[2,1,3,96,96]{4,3,2,1,0:T(8,128)}, u32[]{:S(2)}) copy-start(f32[2,1,3,96,96]{4,3,2,1,0:T(8,128)} %b_ref.1) | copy-start | bytes 663556

commit v3 on v2

--- a/solution.py
+++ b/solution.py
@@ -10,15 +10,15 @@
 MESH = pl.DeviceIdType.MESH
 NX, NY, NZH, NZL, NK = 4, 4, 2, 8, 2
 NZ = NZH * NZL
+LEAPS = NZL // 2
 B, SLOTS, PACK = 96, 3, 72
 CUT = 32
 NB, GROUPS, WIDTH = 128, 8, 16
-ROW = GROUPS * SLOTS
 QUAD = GROUPS // NZH
 DEPTH = QUAD * SLOTS * 128
 
-T_RING, T_TAIL0, T_TAIL, T_FAR = 2.7, 12.0, 3.0, 21.6
-AT_NEAR, AT_LEFT = 29.6, 36.0
+T_RING, T_OWN, T_TAIL0, T_TAIL, T_SIDE0, T_SIDE, T_FAR = 3.6, 13.0, 14.0, 3.0, 18.0, 2.0, 16.0
+AT_NEAR, AT_LEFT = 24.5, 37.0
 
 
 def here():
@@ -66,11 +66,14 @@
     me = here()
     zl, zh, x, y, k = me["zl"], me["zh"], me["x"], me["y"], me["k"]
     z = zh * NZL + zl
-    partners = [moved(me, *step) for step in (
-        ("z", 1), ("z", -1), ("x", 1), ("x", -1), ("x", 2), ("y", 1), ("y", -1), ("y", 2), ("k", 1))]
+    steps = [("z", 1), ("z", -1), ("z", 2), ("z", -2), ("x", 1), ("x", -1), ("x", 2), ("y", 1), ("y", -1), ("y", 2), ("k", 1)]
+    near_by = {step: moved(me, *step) for step in steps}
+    ids = {step: device(at) for step, at in near_by.items()}
+    spots = {(axis, by): near_by[axis, by if by < 3 else -1][axis] if by else me[axis] for axis in ("x", "y") for by in range(4)}
+    ups = [(z + j) % NZ for j in range(NZ)]
     barrier = pltpu.get_barrier_semaphore()
-    for other in partners:
-        pl.semaphore_signal(barrier, inc=1, device_id=device(other), device_id_type=MESH)
+    for step in steps:
+        pl.semaphore_signal(barrier, inc=1, device_id=ids[step], device_id_type=MESH)
     load = pltpu.make_async_copy(b_ref, raw, lsem.at[0])
     load.start()
     load.wait()
@@ -84,14 +87,14 @@
     ]
     for copy in local:
         copy.start()
-    pl.semaphore_wait(barrier, len(partners))
+    pl.semaphore_wait(barrier, len(steps))
 
     sent = []
 
     def send(src, dst, to, sems, index, when=None):
         copy = pltpu.make_async_remote_copy(
             src_ref=src, dst_ref=dst, send_sem=sems.at[(0,) + index], recv_sem=sems.at[(1,) + index],
-            device_id=device(to), device_id_type=MESH)
+            device_id=ids[to], device_id_type=MESH)
         if when is None:
             copy.start()
         else:
@@ -101,17 +104,27 @@
 
     events = []
 
-    ring, tail = {}, {}
-
-    def ring_step(d, n, c):
+    ring, side, tail = {}, {}, {}
+
+    def ring_step(d, m, c):
         way = 1 - 2 * d
-        origin = (z - way * n + NZ) % NZ
-        if n > 0:
-            ring[d, n - 1, c].wait_recv()
-        if n < NZL:
-            src = own.at[d, c] if n == 0 else line.at[origin, d, c]
-            dst = line.at[origin, d, c] if n < NZL - 1 else far.at[d, k, x, y, c]
-            ring[d, n, c] = send(src, dst, moved(me, "z", way), s1sem, (d, n, c))
+        origin = ups[-way * 2 * m % NZ]
+        if m > 0:
+            ring[d, m - 1, c].wait_recv()
+        if m < LEAPS:
+            src = own.at[d, c] if m == 0 else line.at[origin, d, c]
+            dst = line.at[origin, d, c] if m < LEAPS - 1 else far.at[d, k, x, y, c]
+            ring[d, m, c] = send(src, dst, ("z", 2 * way), s1sem, (d, m, c))
+
+    def side_send(d, m, c):
+        way = 1 - 2 * d
+        origin, to = ups[-way * 2 * m % NZ], ups[way % NZ]
+        src = own.at[d, c] if m == 0 else line.at[origin, d, c]
+        side[d, m, c] = send(src, line.at[origin, d, c], ("z", way), s1sem, (d, LEAPS + m, c), origin // NZL == to // NZL)
+
+    def side_wait(d, m, c):
+        way = 1 - 2 * d
+        pl.when(ups[-way * (2 * m + 1) % NZ] // NZL == zh)(side[d, m, c].wait_recv)
 
     def tail_step(d, n, c):
         way = 1 - 2 * d
@@ -124,18 +137,20 @@
             pl.when(got)(tail[d, n - 1, c].wait_recv)
         if n < NZL - 1:
             src = own.at[part, c] if n == 0 else line.at[origin, part, c]
-            tail[d, n, c] = send(src, line.at[origin, part, c], moved(me, "z", way), s2sem, (d, n, c),
+            tail[d, n, c] = send(src, line.at[origin, part, c], ("z", way), s2sem, (d, n, c),
                                  jnp.logical_and(got, more))
 
-    for n in range(NZL):
-        for c in range(SLOTS):
-            for d in range(2):
-                events.append((T_RING * n + 0.76 * c, functools.partial(ring_step, d, n, c)))
-                events.append((2.3 if n == 0 else T_TAIL0 + T_TAIL * n + 0.76 * c, functools.partial(tail_step, d, n, c)))
+    for c in range(SLOTS):
+        for d in range(2):
+            for m in range(LEAPS):
+                events.append((T_RING * m + 0.76 * c, functools.partial(ring_step, d, m, c)))
+                events.append((T_SIDE0 + T_SIDE * m + 0.76 * c, functools.partial(side_send, d, m, c)))
+                events.append((T_SIDE0 + T_SIDE * m + 8.0 + 0.76 * c, functools.partial(side_wait, d, m, c)))
+            for n in range(NZL):
+                events.append((T_OWN if n == 0 else T_TAIL0 + T_TAIL * n + 0.76 * c, functools.partial(tail_step, d, n, c)))
 
     def plane(phase, store, start):
         first, second = ("x", "y"), ("y", "x")
-        size = {"x": NX, "y": NY}
         chunks = {}
 
         def ref(ab, p, q, d=None):
@@ -146,11 +161,11 @@
             return view.at[:, pl.ds(0, low)] if d == 0 else view.at[:, pl.ds(low, PACK - low)]
 
         def spot(axis, by):
-            return (me[axis] + by + size[axis]) % size[axis]
+            return spots[axis, by % 4]
 
         def go(ab, p, q, axis, way, sem, d=None):
             r = ref(ab, p, q, d)
-            return send(r, r, moved(me, axis, way), xsem, (phase, ab, sem))
+            return send(r, r, (axis, way), xsem, (phase, ab, sem))
 
         def spread(ab, j):
             a, b = first[ab], second[ab]
@@ -161,7 +176,7 @@
             a = first[ab]
             if phase == 1:
                 for c in range(SLOTS):
-                    ring_step(ab, NZL, c)
+                    ring_step(ab, LEAPS, c)
             for d, way in enumerate((1, -1, 2)):
                 chunks[ab, "a", d] = go(ab, me[a], me[second[ab]], a, way, d)
 
@@ -180,7 +195,7 @@
                 chunks[ab, "b2", j, d].wait_recv()
             p = spot(first[ab], j)
             src = store.at[ab, k, p] if ab == 0 else store.at[ab, k, :, p]
-            chunks[ab, "c", j] = send(src, src, moved(me, "k", 1), dsem, (phase, ab, j))
+            chunks[ab, "c", j] = send(src, src, ("k", 1), dsem, (phase, ab, j))
 
         def finish(ab, j):
             chunks[ab, "c", j].wait_recv()
@@ -206,25 +221,28 @@
 
     first_row = lax.axis_index("row") * WIDTH + lax.axis_index("layer") * 2
 
+    def held(block_row, group, slot):
+        return table[(slot * GROUPS + group) * NB + block_row]
+
     def left_side(i, half, h, g4):
+        free = jnp.zeros((B, 128 - B), jnp.bfloat16)
         for t in range(SLOTS):
             high, low = split(unpack(line[zh * NZL + h * QUAD + g4, i, t]))
-            lanes = pl.ds(pl.multiple_of((g4 * SLOTS + t) * 128, 128), B)
-            lhs[i, half, 0:B, lanes] = high
-            lhs[i, half, B:2 * B, lanes] = low
-
-    def right_side(i, half, h, g4):
+            lanes = pl.ds(pl.multiple_of((g4 * SLOTS + t) * 128, 128), 128)
+            lhs[i, half, 0:B, lanes] = jnp.concatenate([high, free], axis=1)
+            lhs[i, half, B:2 * B, lanes] = jnp.concatenate([low, free], axis=1)
+
+    def right_side(slots, i, half, h, g4):
         store = near if half == 0 else far
-        base = (first_row + i) * ROW
+        block_row = first_row + i
         group = h * QUAD + g4
-        wanted = [table[base + zl * SLOTS + s] for s in range(SLOTS)]
+        wanted = {s: held(block_row, zl, s) for s in slots}
         for t in range(SLOTS):
-            col = table[base + group * SLOTS + t]
+            col = held(block_row, group, t)
             inner = jnp.maximum(col, 0)
-            at = (group * WIDTH + inner) * ROW + zl * SLOTS
-            cols = [table[at + u] for u in range(SLOTS)]
+            cols = [held(group * WIDTH + inner, zl, u) for u in range(SLOTS)]
             depth = pl.ds(pl.multiple_of((g4 * SLOTS + t) * 128, 128), B)
-            for s in range(SLOTS):
+            for s in slots:
                 want = jnp.where(col >= 0, wanted[s] + 1, 0)
                 hits = [jnp.where(cols[u] + 1 == want, 1, 0) * jnp.where(want > 0, 1, 0) for u in range(SLOTS)]
                 u = jnp.minimum(hits[1] + 2 * hits[2], SLOTS - 1)
@@ -234,27 +252,25 @@
                 rhs_hi[i, half, depth, s * 128:s * 128 + B] = high
                 rhs_lo[i, half, depth, s * 128:s * 128 + B] = low
 
-    def multiply(i, half):
+    def multiply(slots, i, half):
         dot = functools.partial(jnp.dot, preferred_element_type=jnp.float32)
-        main = dot(lhs[i, half], rhs_hi[i, half])
-        rest = dot(lhs[i, half, 0:B, :], rhs_lo[i, half])
+        lanes = slice(slots[0] * 128, (slots[-1] + 1) * 128)
+        main = dot(lhs[i, half], rhs_hi[i, half, :, lanes])
+        rest = dot(lhs[i, half, 0:B, :], rhs_lo[i, half, :, lanes])
         value = main[0:B] + (main[B:] + rest)
-        for s in range(SLOTS):
-            part = value[:, s * 128:s * 128 + B]
+        for n, s in enumerate(slots):
+            part = value[:, n * 128:n * 128 + B]
             if half == 0:
                 out_ref[i, 0, s] = part
             else:
                 out_ref[i, 0, s] += part
 
-    def clear(ref):
-        ref[...] = jnp.zeros_like(ref)
-
     def prepare():
-        for i in range(2):
-            for half in range(2):
-                clear(lhs.at[i, half])
-                clear(rhs_hi.at[i, half])
-                clear(rhs_lo.at[i, half])
+        for ref in (rhs_hi, rhs_lo):
+            for i in range(2):
+                for half in range(2):
+                    for n in range(QUAD * SLOTS):
+                        ref[i, half, n * 128 + B:(n + 1) * 128, :] = jnp.zeros((128 - B, SLOTS * 128), jnp.bfloat16)
 
     def every(fn, half, h):
         def step(n, _):
@@ -263,31 +279,24 @@
         lax.fori_loop(0, 2 * QUAD, step, 0)
 
     other = 1 - zh
+    first, rest, whole = (0,), (1, 2), (0, 1, 2)
     events.append((0.3, prepare))
-    events.append((AT_NEAR, lambda: every(right_side, 0, zh)))
+    events.append((AT_NEAR, lambda: every(functools.partial(right_side, whole), 0, zh)))
     events.append((AT_LEFT, lambda: every(left_side, 0, zh)))
-    events.append((AT_LEFT + 1.5, lambda: every(left_side, 1, other)))
+    events.append((AT_LEFT + 0.5, lambda: every(left_side, 1, other)))
     for i in range(2):
-        events.append((AT_LEFT + 2.5 + i, functools.partial(multiply, i, 0)))
+        events.append((AT_LEFT + 1.0 + i, functools.partial(multiply, whole, i, 0)))
     for _, step in sorted(events, key=lambda e: e[0]):
         step()
-    every(right_side, 1, other)
-    for i in range(2):
-        multiply(i, 1)
-
-    row, col = lax.axis_index("row"), lax.axis_index("col")
-    diagonal = row == col
+
+    def far_products(slots):
+        every(functools.partial(right_side, slots), 1, other)
+        for i in range(2):
+            multiply(slots, i, 1)
+
+    far_products(first)
+    diagonal = lax.axis_index("row") == lax.axis_index("col")
     n_yk = NY * NK
-    def own_trace():
-        eye = lax.broadcasted_iota(jnp.int32, (B, B), 0) == lax.broadcasted_iota(jnp.int32, (B, B), 1)
-        total = jnp.zeros((1, B), jnp.float32)
-        for i in range(2):
-            for s in range(SLOTS):
-                at = first_row + i
-                on = table[at * ROW + zl * SLOTS + s] == at % WIDTH
-                total += jnp.sum(jnp.where(eye, out_ref[i, 0, s], 0.0), axis=0, keepdims=True) * jnp.where(on, 1.0, 0.0)
-        one[...] = jnp.full((8, 128), jnp.sum(total), jnp.float32)
-
     mine = y * NK + k
 
     def plane_copy(j):
@@ -297,55 +306,55 @@
             src_ref=one, dst_ref=in_plane.at[mine], send_sem=psem.at[0, j], recv_sem=psem.at[1, j],
             device_id=device(to), device_id_type=MESH)
 
-    n_plane = NX * n_yk
-    plane_copies = [plane_copy(j) for j in range(n_plane) if j != 3 * n_yk]
+    plane_copies = [plane_copy(j) for j in range(NX * n_yk) if j != 3 * n_yk]
 
     @pl.when(diagonal)
     def _():
-        own_trace()
+        eye = lax.broadcasted_iota(jnp.int32, (B, B), 0) == lax.broadcasted_iota(jnp.int32, (B, B), 1)
+        total = jnp.sum(jnp.where(eye, out_ref[0, 0, 0] + out_ref[1, 0, 0], 0.0))
+        one[...] = jnp.full((8, 128), total, jnp.float32)
         for copy in plane_copies:
             copy.start()
         in_plane[mine] = one[...]
 
+    far_products(rest)
+
     holds = zh == zl // NX
     dx_in = (x - zl % NX + NX) % NX
-    for slot, dx in enumerate((2, 1, 3, 0)):
+    for n, dx in enumerate((2, 1, 3, 0)):
         @pl.when(jnp.logical_and(holds, dx_in == dx))
         def _():
             for t in range(n_yk):
                 if dx != 0 or t != 0:
-                    plane_copy(slot * n_yk + t).wait_recv()
-
-    def z_copy(j):
-        return pltpu.make_async_remote_copy(
-            src_ref=two, dst_ref=along.at[zl], send_sem=zsem.at[0, j], recv_sem=zsem.at[1, j],
-            device_id=device(moved(me, "z", j)), device_id_type=MESH)
-
-    z_order = sorted(range(1, NZ), key=lambda j: -min(j, NZ - j))
+                    plane_copies[n * n_yk + t - (dx == 0)].wait_recv()
+
+    z_copies = {j: pltpu.make_async_remote_copy(
+        src_ref=two, dst_ref=along.at[zl], send_sem=zsem.at[0, j], recv_sem=zsem.at[1, j],
+        device_id=device(moved(me, "z", j)), device_id_type=MESH)
+        for j in sorted(range(1, NZ), key=lambda j: -min(j, NZ - j))}
 
     @pl.when(holds)
     def _():
         two[...] = jnp.sum(in_plane[...], axis=0)
-        for j in z_order:
-            z_copy(j).start()
+        for copy in z_copies.values():
+            copy.start()
         along[zl] = two[...]
 
-    for j in range(1, NZ):
-        zs = (z - j + NZ) % NZ
-        @pl.when(zs // NZL == zs % NZL // NX)
-        def _():
-            z_copy(j).wait_recv()
-    trace_ref[...] = jnp.sum(along[...], axis=0)
+    for j, copy in z_copies.items():
+        from_z = ups[-j % NZ]
+        pl.when(from_z // NZL == from_z % NZL // NX)(copy.wait_recv)
+    trace_ref[0, 0] = jnp.sum(along[:, 0:1, 0:1])
 
     @pl.when(holds)
     def _():
-        for j in z_order:
-            z_copy(j).wait_send()
+        for copy in z_copies.values():
+            copy.wait_send()
 
     @pl.when(diagonal)
     def _():
         for copy in plane_copies:
             copy.wait_send()
+
     for copy, when in sent:
         if when is None:
             copy.wait_send()
@@ -356,9 +365,9 @@
 def square(table, blocks, collective_id=0, name="square"):
     return pl.pallas_call(
         kernel,
-        out_shape=(jax.ShapeDtypeStruct((2, 1, SLOTS, B, B), jnp.float32), jax.ShapeDtypeStruct((8, 128), jnp.float32)),
+        out_shape=(jax.ShapeDtypeStruct((2, 1, SLOTS, B, B), jnp.float32), jax.ShapeDtypeStruct((1, 1), jnp.float32)),
         in_specs=[pl.BlockSpec(memory_space=pltpu.SMEM), pl.BlockSpec(memory_space=pl.ANY)],
-        out_specs=(pl.BlockSpec(memory_space=pltpu.VMEM), pl.BlockSpec(memory_space=pltpu.VMEM)),
+        out_specs=(pl.BlockSpec(memory_space=pltpu.VMEM), pl.BlockSpec(memory_space=pltpu.SMEM)),
         scratch_shapes=[
             pltpu.VMEM((2, 1, SLOTS, B, B), jnp.float32),
             pltpu.VMEM((2, SLOTS, PACK, 128), jnp.float32),
@@ -386,7 +395,7 @@
 
 
 def body(blocks, block_cols, occupancy):
-    table = jnp.where(occupancy == 1, block_cols, -1).reshape(-1)
+    table = jnp.where(occupancy == 1, block_cols, -1).transpose(2, 1, 0).reshape(-1)
     product, trace = square(table, blocks)
     return product, trace[0, 0]
 

time: 90.5 us -> 88.2 us (0.975)
  Pallas kernels: 86.4 us -> 83.1 us
  between operations: 0.65 us -> 2.4 us
    pallas_call x1, Pallas kernels: 86.4 us -> 83.1 us  [square(): pl.pallas_call(kernel, out_shape=(jax.ShapeDtypeStruct((2, 1, SLOTS, B, B...]
where the time goes in v3:
time: 88.2 us; the launch traced here: 87.9 us
  Pallas kernels  83.1 us (94%)
  between operations  2.4 us (3%)
  local copies, waits for them, and re-layouts  1.68 us (2%)
    pallas_call x1, Pallas kernels, square(): pl.pallas_call(kernel, out_shape=(jax.ShapeDtypeStruct((2, 1, SLOTS, B, B...  83.1 us

profile of v3, /device:TPU:1, one launch (start us, length us, event | category | flops | bytes accessed | tf_op | source)
XLA Modules:
  0.0 87.9 jit_solution(1803450738666523412)
XLA Ops:
  0.6 0.7 select_bitcast_fusion.table
  1.4 0.0 copy-start
  1.4 1.0 %copy-done = f32[2,1,3,96,96]{4,3,2,1,0:T(8,128)S(1)} copy-done((f32[2,1,3,96,96]{4,3,2,1,0:T(8,128)S(1)}, f32[2,1,3,96,96]{4,3,2,1,0:T(8,128)}, u32[]{:S(2)}) %copy-start) | copy-done | bytes 221208
  2.3 83.1 %square.1 = (f32[2,1,3,96,96]{4,3,2,1,0:T(8,128)S(1)}, f32[1,1]{1,0:T(1,128)}) custom-call(s32[3072]{0:T(1024)S(1)} %select_bitcast_fusion.table, f32[2,1,3,96,96]{4,3,2,1,0:T(8,128)S(1)} %copy-done), custom_call_target="tpu_custom_call" | custom-call | tf_op jit(solution)/shard_map/square/pallas_call | solution.py:366
  85.4 0.7 copy.7
Async XLA Ops:
  1.4 1.0 %copy-start = (f32[2,1,3,96,96]{4,3,2,1,0:T(8,128)S(1)}, f32[2,1,3,96,96]{4,3,2,1,0:T(8,128)}, u32[]{:S(2)}) copy-start(f32[2,1,3,96,96]{4,3,2,1,0:T(8,128)} %b_ref.1) | copy-start | bytes 663556

commit v4 on v3

--- a/solution.py
+++ b/solution.py
@@ -18,7 +18,7 @@
 DEPTH = QUAD * SLOTS * 128
 
 T_RING, T_OWN, T_TAIL0, T_TAIL, T_SIDE0, T_SIDE, T_FAR = 3.6, 13.0, 14.0, 3.0, 18.0, 2.0, 16.0
-AT_NEAR, AT_LEFT = 24.5, 37.0
+AT_NEAR, AT_TRACE, AT_LEFT = 24.5, 30.0, 37.0
 
 
 def here():
@@ -61,7 +61,7 @@
     return high, (value - high.astype(jnp.float32)).astype(jnp.bfloat16)
 
 
-def kernel(table, b_ref, out_ref, trace_ref, raw, own, line, near, far, lhs, rhs_hi, rhs_lo, in_plane, along, one, two,
+def kernel(table, b_ref, out_ref, trace_ref, raw, own, line, near, far, lhs, rhs_hi, rhs_lo, in_plane, along, one, two, near_sum,
            lsem, s1sem, s2sem, xsem, dsem, psem, zsem):
     me = here()
     zl, zh, x, y, k = me["zl"], me["zh"], me["x"], me["y"], me["k"]
@@ -278,10 +278,67 @@
             return 0
         lax.fori_loop(0, 2 * QUAD, step, 0)
 
+    diagonal = lax.axis_index("row") == lax.axis_index("col")
+    holds = zh == zl // NX
+    n_yk = NY * NK
+    mine = y * NK + k
+
+    def plane_copy(j):
+        dx, t = (2, 1, 3, 0)[j // n_yk], (mine + j % n_yk) % n_yk
+        to = {"x": (x + dx) % NX, "y": t // NK, "k": t % NK, "zh": zh, "zl": zl}
+        return pltpu.make_async_remote_copy(
+            src_ref=one, dst_ref=in_plane.at[mine], send_sem=psem.at[0, j], recv_sem=psem.at[1, j],
+            device_id=device(to), device_id_type=MESH)
+
+    plane_copies = [plane_copy(j) for j in range(NX * n_yk) if j != 3 * n_yk]
+    z_copies = {j: pltpu.make_async_remote_copy(
+        src_ref=two, dst_ref=along.at[zl], send_sem=zsem.at[0, j], recv_sem=zsem.at[1, j],
+        device_id=device(moved(me, "z", j)), device_id_type=MESH)
+        for j in sorted(range(1, NZ), key=lambda j: -min(j, NZ - j))}
+
+    def diagonal_sum():
+        eye = lax.broadcasted_iota(jnp.int32, (B, B), 0) == lax.broadcasted_iota(jnp.int32, (B, B), 1)
+        total = jnp.sum(jnp.where(eye, out_ref[0, 0, 0] + out_ref[1, 0, 0], 0.0))
+        return jnp.full((8, 128), total, jnp.float32)
+
+    def to_plane():
+        for copy in plane_copies:
+            copy.start()
+        in_plane[mine] = one[...]
+
+    def to_line():
+        dx_in = (x - zl % NX + NX) % NX
+        for n, dx in enumerate((2, 1, 3, 0)):
+            @pl.when(dx_in == dx)
+            def _():
+                for t in range(n_yk):
+                    if dx != 0 or t != 0:
+                        plane_copies[n * n_yk + t - (dx == 0)].wait_recv()
+        two[...] = jnp.sum(in_plane[...], axis=0)
+        for copy in z_copies.values():
+            copy.start()
+        along[zl] = two[...]
+
     other = 1 - zh
     first, rest, whole = (0,), (1, 2), (0, 1, 2)
+
+    def early_trace():
+        @pl.when(diagonal)
+        def _():
+            every(left_side, 0, zh)
+            for i in range(2):
+                multiply(first, i, 0)
+            near_sum[...] = diagonal_sum()
+
+            @pl.when(zh == 1)
+            def _():
+                one[...] = near_sum[...]
+                to_plane()
+
     events.append((0.3, prepare))
     events.append((AT_NEAR, lambda: every(functools.partial(right_side, whole), 0, zh)))
+    events.append((AT_TRACE, early_trace))
+    events.append((AT_TRACE + 3.0, lambda: pl.when(jnp.logical_and(holds, zh == 1))(to_line)))
     events.append((AT_LEFT, lambda: every(left_side, 0, zh)))
     events.append((AT_LEFT + 0.5, lambda: every(left_side, 1, other)))
     for i in range(2):
@@ -295,50 +352,14 @@
             multiply(slots, i, 1)
 
     far_products(first)
-    diagonal = lax.axis_index("row") == lax.axis_index("col")
-    n_yk = NY * NK
-    mine = y * NK + k
-
-    def plane_copy(j):
-        dx, t = (2, 1, 3, 0)[j // n_yk], (mine + j % n_yk) % n_yk
-        to = {"x": (x + dx) % NX, "y": t // NK, "k": t % NK, "zh": zh, "zl": zl}
-        return pltpu.make_async_remote_copy(
-            src_ref=one, dst_ref=in_plane.at[mine], send_sem=psem.at[0, j], recv_sem=psem.at[1, j],
-            device_id=device(to), device_id_type=MESH)
-
-    plane_copies = [plane_copy(j) for j in range(NX * n_yk) if j != 3 * n_yk]
-
-    @pl.when(diagonal)
+
+    @pl.when(jnp.logical_and(diagonal, zh == 0))
     def _():
-        eye = lax.broadcasted_iota(jnp.int32, (B, B), 0) == lax.broadcasted_iota(jnp.int32, (B, B), 1)
-        total = jnp.sum(jnp.where(eye, out_ref[0, 0, 0] + out_ref[1, 0, 0], 0.0))
-        one[...] = jnp.full((8, 128), total, jnp.float32)
-        for copy in plane_copies:
-            copy.start()
-        in_plane[mine] = one[...]
+        one[...] = 2.0 * diagonal_sum() - near_sum[...]
+        to_plane()
 
     far_products(rest)
-
-    holds = zh == zl // NX
-    dx_in = (x - zl % NX + NX) % NX
-    for n, dx in enumerate((2, 1, 3, 0)):
-        @pl.when(jnp.logical_and(holds, dx_in == dx))
-        def _():
-            for t in range(n_yk):
-                if dx != 0 or t != 0:
-                    plane_copies[n * n_yk + t - (dx == 0)].wait_recv()
-
-    z_copies = {j: pltpu.make_async_remote_copy(
-        src_ref=two, dst_ref=along.at[zl], send_sem=zsem.at[0, j], recv_sem=zsem.at[1, j],
-        device_id=device(moved(me, "z", j)), device_id_type=MESH)
-        for j in sorted(range(1, NZ), key=lambda j: -min(j, NZ - j))}
-
-    @pl.when(holds)
-    def _():
-        two[...] = jnp.sum(in_plane[...], axis=0)
-        for copy in z_copies.values():
-            copy.start()
-        along[zl] = two[...]
+    pl.when(jnp.logical_and(holds, zh == 0))(to_line)
 
     for j, copy in z_copies.items():
         from_z = ups[-j % NZ]
@@ -381,6 +402,7 @@
             pltpu.VMEM((NZL, 8, 128), jnp.float32),
             pltpu.VMEM((8, 128), jnp.float32),
             pltpu.VMEM((8, 128), jnp.float32),
+            pltpu.VMEM((8, 128), jnp.float32),
             pltpu.SemaphoreType.DMA((3,)),
             pltpu.SemaphoreType.DMA((2, 2, NZL, SLOTS)),
             pltpu.SemaphoreType.DMA((2, 2, NZL, SLOTS)),

time: 88.2 us -> 86.8 us (0.984)
  Pallas kernels: 83.1 us -> 81.7 us
    pallas_call x1, Pallas kernels: 83.1 us -> 81.7 us  [square(): pl.pallas_call(kernel, out_shape=(jax.ShapeDtypeStruct((2, 1, SLOTS, B, B...]
where the time goes in v4:
time: 86.8 us; the launch traced here: 86.5 us
  Pallas kernels  81.7 us (94%)
  between operations  2.4 us (3%)
  local copies, waits for them, and re-layouts  1.68 us (2%)
    pallas_call x1, Pallas kernels, square(): pl.pallas_call(kernel, out_shape=(jax.ShapeDtypeStruct((2, 1, SLOTS, B, B...  81.7 us

profile of v4, /device:TPU:1, one launch (start us, length us, event | category | flops | bytes accessed | tf_op | source)
XLA Modules:
  0.0 86.5 jit_solution(12098604020156009846)
XLA Ops:
  0.6 0.7 select_bitcast_fusion.table
  1.4 0.0 copy-start
  1.4 1.0 %copy-done = f32[2,1,3,96,96]{4,3,2,1,0:T(8,128)S(1)} copy-done((f32[2,1,3,96,96]{4,3,2,1,0:T(8,128)S(1)}, f32[2,1,3,96,96]{4,3,2,1,0:T(8,128)}, u32[]{:S(2)}) %copy-start) | copy-done | bytes 221208
  2.3 81.7 %square.1 = (f32[2,1,3,96,96]{4,3,2,1,0:T(8,128)S(1)}, f32[1,1]{1,0:T(1,128)}) custom-call(s32[3072]{0:T(1024)S(1)} %select_bitcast_fusion.table, f32[2,1,3,96,96]{4,3,2,1,0:T(8,128)S(1)} %copy-done), custom_call_target="tpu_custom_call" | custom-call | tf_op jit(solution)/shard_map/square/pallas_call | solution.py:387
  84.0 0.7 copy.7
Async XLA Ops:
  1.4 1.0 %copy-start = (f32[2,1,3,96,96]{4,3,2,1,0:T(8,128)S(1)}, f32[2,1,3,96,96]{4,3,2,1,0:T(8,128)}, u32[]{:S(2)}) copy-start(f32[2,1,3,96,96]{4,3,2,1,0:T(8,128)} %b_ref.1) | copy-start | bytes 663556

commit v5 on v4

--- a/solution.py
+++ b/solution.py
@@ -62,7 +62,8 @@
 
 
 def kernel(table, b_ref, out_ref, trace_ref, raw, own, line, near, far, lhs, rhs_hi, rhs_lo, in_plane, along, one, two, near_sum,
-           lsem, s1sem, s2sem, xsem, dsem, psem, zsem):
+           ruler,
+           lsem, ring_in, side_in, tail_in, plane_in, share_in, small_in, out_sem, side_out, tail_out):
     me = here()
     zl, zh, x, y, k = me["zl"], me["zh"], me["x"], me["y"], me["k"]
     z = zh * NZL + zl
@@ -81,30 +82,37 @@
         for s in range(SLOTS):
             own[i, s] = pack(raw[i, 0, s])
     local = [
-        pltpu.make_async_copy(own, line.at[z], lsem.at[0]),
-        pltpu.make_async_copy(own.at[0], near.at[0, k, x, y], lsem.at[1]),
-        pltpu.make_async_copy(own.at[1], near.at[1, k, x, y], lsem.at[2]),
+        pltpu.make_async_copy(own, line.at[z], lsem.at[1]),
+        pltpu.make_async_copy(own.at[0], near.at[0, k, x, y], lsem.at[2]),
+        pltpu.make_async_copy(own.at[1], near.at[1, k, x, y], lsem.at[3]),
     ]
     for copy in local:
         copy.start()
     pl.semaphore_wait(barrier, len(steps))
 
-    sent = []
-
-    def send(src, dst, to, sems, index, when=None):
+    def send(src, dst, to, out, into, when=None):
         copy = pltpu.make_async_remote_copy(
-            src_ref=src, dst_ref=dst, send_sem=sems.at[(0,) + index], recv_sem=sems.at[(1,) + index],
-            device_id=ids[to], device_id_type=MESH)
+            src_ref=src, dst_ref=dst, send_sem=out, recv_sem=into, device_id=ids[to], device_id_type=MESH)
         if when is None:
             copy.start()
         else:
             pl.when(when)(copy.start)
-        sent.append((copy, when))
         return copy
 
+    def drain(sem, view, when=None):
+        def wait():
+            pltpu.make_async_copy(view, view, sem).wait()
+        if when is None:
+            wait()
+        else:
+            pl.when(when)(wait)
+
+    three, six = line.at[0, 0], line.at[0]
+    after = []
+
     events = []
 
-    ring, side, tail = {}, {}, {}
+    ring, tail = {}, {}
 
     def ring_step(d, m, c):
         way = 1 - 2 * d
@@ -114,17 +122,20 @@
         if m < LEAPS:
             src = own.at[d, c] if m == 0 else line.at[origin, d, c]
             dst = line.at[origin, d, c] if m < LEAPS - 1 else far.at[d, k, x, y, c]
-            ring[d, m, c] = send(src, dst, ("z", 2 * way), s1sem, (d, m, c))
+            ring[d, m, c] = send(src, dst, ("z", 2 * way), out_sem.at[0], ring_in.at[d, m, c])
 
     def side_send(d, m, c):
         way = 1 - 2 * d
         origin, to = ups[-way * 2 * m % NZ], ups[way % NZ]
         src = own.at[d, c] if m == 0 else line.at[origin, d, c]
-        side[d, m, c] = send(src, line.at[origin, d, c], ("z", way), s1sem, (d, LEAPS + m, c), origin // NZL == to // NZL)
-
-    def side_wait(d, m, c):
+        when = origin // NZL == to // NZL
+        send(src, line.at[origin, d, c], ("z", way), side_out.at[d, m], side_in.at[d, m], when)
+        if c == SLOTS - 1:
+            after.append((side_out.at[d, m], three, when))
+
+    def side_wait(d, m):
         way = 1 - 2 * d
-        pl.when(ups[-way * (2 * m + 1) % NZ] // NZL == zh)(side[d, m, c].wait_recv)
+        drain(side_in.at[d, m], three, ups[-way * (2 * m + 1) % NZ] // NZL == zh)
 
     def tail_step(d, n, c):
         way = 1 - 2 * d
@@ -137,21 +148,23 @@
             pl.when(got)(tail[d, n - 1, c].wait_recv)
         if n < NZL - 1:
             src = own.at[part, c] if n == 0 else line.at[origin, part, c]
-            tail[d, n, c] = send(src, line.at[origin, part, c], ("z", way), s2sem, (d, n, c),
-                                 jnp.logical_and(got, more))
+            when = jnp.logical_and(got, more)
+            tail[d, n, c] = send(src, line.at[origin, part, c], ("z", way), tail_out.at[d, n], tail_in.at[d, n, c], when)
+            if c == SLOTS - 1:
+                after.append((tail_out.at[d, n], three, when))
 
     for c in range(SLOTS):
         for d in range(2):
             for m in range(LEAPS):
                 events.append((T_RING * m + 0.76 * c, functools.partial(ring_step, d, m, c)))
                 events.append((T_SIDE0 + T_SIDE * m + 0.76 * c, functools.partial(side_send, d, m, c)))
-                events.append((T_SIDE0 + T_SIDE * m + 8.0 + 0.76 * c, functools.partial(side_wait, d, m, c)))
+                if c == SLOTS - 1:
+                    events.append((T_SIDE0 + T_SIDE * m + 8.0 + 0.76 * c, functools.partial(side_wait, d, m)))
             for n in range(NZL):
                 events.append((T_OWN if n == 0 else T_TAIL0 + T_TAIL * n + 0.76 * c, functools.partial(tail_step, d, n, c)))
 
     def plane(phase, store, start):
         first, second = ("x", "y"), ("y", "x")
-        chunks = {}
 
         def ref(ab, p, q, d=None):
             view = store.at[ab, k, p, q] if ab == 0 else store.at[ab, k, q, p]
@@ -165,12 +178,12 @@
 
         def go(ab, p, q, axis, way, sem, d=None):
             r = ref(ab, p, q, d)
-            return send(r, r, (axis, way), xsem, (phase, ab, sem))
+            send(r, r, (axis, way), out_sem.at[1 + phase], plane_in.at[phase, ab, sem])
 
         def spread(ab, j):
             a, b = first[ab], second[ab]
-            for d, way in enumerate((1, -1)):
-                chunks[ab, "b", j, d] = go(ab, spot(a, j), me[b], b, way, 3 + 4 * j + d)
+            for way in (1, -1):
+                go(ab, spot(a, j), me[b], b, way, 3 + j)
 
         def begin(ab):
             a = first[ab]
@@ -178,27 +191,23 @@
                 for c in range(SLOTS):
                     ring_step(ab, LEAPS, c)
             for d, way in enumerate((1, -1, 2)):
-                chunks[ab, "a", d] = go(ab, me[a], me[second[ab]], a, way, d)
+                go(ab, me[a], me[second[ab]], a, way, d)
 
         def pass_on(ab, d):
-            chunks[ab, "a", d].wait_recv()
+            drain(plane_in.at[phase, ab, d], three)
             spread(ab, (3, 1, 2)[d])
 
         def pass_second(ab, j):
             a, b = first[ab], second[ab]
+            drain(plane_in.at[phase, ab, 3 + j], six)
             for d, way in enumerate((1, -1)):
-                chunks[ab, "b", j, d].wait_recv()
-                chunks[ab, "b2", j, d] = go(ab, spot(a, j), spot(b, -way), b, way, 5 + 4 * j + d, d)
+                go(ab, spot(a, j), spot(b, -way), b, way, 7 + j, d)
 
         def share(ab, j):
-            for d in range(2):
-                chunks[ab, "b2", j, d].wait_recv()
+            drain(plane_in.at[phase, ab, 7 + j], three)
             p = spot(first[ab], j)
             src = store.at[ab, k, p] if ab == 0 else store.at[ab, k, :, p]
-            chunks[ab, "c", j] = send(src, src, ("k", 1), dsem, (phase, ab, j))
-
-        def finish(ab, j):
-            chunks[ab, "c", j].wait_recv()
+            send(src, src, ("k", 1), out_sem.at[3 + phase], share_in.at[phase])
 
         order = [
             (0.0, begin), (0.01, lambda ab: spread(ab, 0)),
@@ -208,11 +217,12 @@
             (15.8, lambda ab: share(ab, 0)), (18.1, lambda ab: share(ab, 3)),
             (18.2, lambda ab: pass_second(ab, 2)), (20.4, lambda ab: share(ab, 1)), (22.6, lambda ab: share(ab, 2)),
         ]
-        for j in range(4):
-            order.append((24.0 if phase == 0 else 1000.0, lambda ab, j=j: finish(ab, j)))
         for at, step in order:
             for ab in range(2):
                 events.append((start + at, functools.partial(step, ab)))
+        events.append((start + 24.0 if phase == 0 else 1000.0, lambda: drain(share_in.at[phase], line)))
+        after.append((out_sem.at[1 + phase], line.at[pl.ds(0, 15)], None))
+        after.append((out_sem.at[3 + phase], line, None))
 
     for copy in local:
         copy.wait()
@@ -287,12 +297,12 @@
         dx, t = (2, 1, 3, 0)[j // n_yk], (mine + j % n_yk) % n_yk
         to = {"x": (x + dx) % NX, "y": t // NK, "k": t % NK, "zh": zh, "zl": zl}
         return pltpu.make_async_remote_copy(
-            src_ref=one, dst_ref=in_plane.at[mine], send_sem=psem.at[0, j], recv_sem=psem.at[1, j],
+            src_ref=one, dst_ref=in_plane.at[mine], send_sem=out_sem.at[5], recv_sem=small_in.at[0],
             device_id=device(to), device_id_type=MESH)
 
     plane_copies = [plane_copy(j) for j in range(NX * n_yk) if j != 3 * n_yk]
     z_copies = {j: pltpu.make_async_remote_copy(
-        src_ref=two, dst_ref=along.at[zl], send_sem=zsem.at[0, j], recv_sem=zsem.at[1, j],
+        src_ref=two, dst_ref=along.at[zl], send_sem=out_sem.at[6], recv_sem=small_in.at[1],
         device_id=device(moved(me, "z", j)), device_id_type=MESH)
         for j in sorted(range(1, NZ), key=lambda j: -min(j, NZ - j))}
 
@@ -307,13 +317,8 @@
         in_plane[mine] = one[...]
 
     def to_line():
-        dx_in = (x - zl % NX + NX) % NX
-        for n, dx in enumerate((2, 1, 3, 0)):
-            @pl.when(dx_in == dx)
-            def _():
-                for t in range(n_yk):
-                    if dx != 0 or t != 0:
-                        plane_copies[n * n_yk + t - (dx == 0)].wait_recv()
+        drain(small_in.at[0], ruler.at[pl.ds(0, n_yk)], jnp.logical_not(diagonal))
+        drain(small_in.at[0], ruler.at[pl.ds(0, n_yk - 1)], diagonal)
         two[...] = jnp.sum(in_plane[...], axis=0)
         for copy in z_copies.values():
             copy.start()
@@ -361,26 +366,15 @@
     far_products(rest)
     pl.when(jnp.logical_and(holds, zh == 0))(to_line)
 
-    for j, copy in z_copies.items():
-        from_z = ups[-j % NZ]
-        pl.when(from_z // NZL == from_z % NZL // NX)(copy.wait_recv)
+    drain(small_in.at[1], ruler.at[pl.ds(0, NZL)], jnp.logical_not(holds))
+    drain(small_in.at[1], ruler.at[pl.ds(0, NZL - 1)], holds)
     trace_ref[0, 0] = jnp.sum(along[:, 0:1, 0:1])
 
-    @pl.when(holds)
-    def _():
-        for copy in z_copies.values():
-            copy.wait_send()
-
-    @pl.when(diagonal)
-    def _():
-        for copy in plane_copies:
-            copy.wait_send()
-
-    for copy, when in sent:
-        if when is None:
-            copy.wait_send()
-        else:
-            pl.when(when)(copy.wait_send)
+    drain(out_sem.at[5], ruler.at[pl.ds(0, NX * n_yk - 1)], diagonal)
+    drain(out_sem.at[6], ruler.at[pl.ds(0, NZ - 1)], holds)
+    drain(out_sem.at[0], line.at[pl.ds(0, LEAPS)])
+    for sem, view, when in after:
+        drain(sem, view, when)
 
 
 def square(table, blocks, collective_id=0, name="square"):
@@ -403,13 +397,17 @@
             pltpu.VMEM((8, 128), jnp.float32),
             pltpu.VMEM((8, 128), jnp.float32),
             pltpu.VMEM((8, 128), jnp.float32),
-            pltpu.SemaphoreType.DMA((3,)),
-            pltpu.SemaphoreType.DMA((2, 2, NZL, SLOTS)),
-            pltpu.SemaphoreType.DMA((2, 2, NZL, SLOTS)),
-            pltpu.SemaphoreType.DMA((2, 2, 2, 20)),
-            pltpu.SemaphoreType.DMA((2, 2, 2, 4)),
-            pltpu.SemaphoreType.DMA((2, NX * NY * NK)),
-            pltpu.SemaphoreType.DMA((2, NZ)),
+            pltpu.VMEM((NX * NY * NK, 8, 128), jnp.float32),
+            pltpu.SemaphoreType.DMA((4,)),
+            pltpu.SemaphoreType.DMA((2, LEAPS, SLOTS)),
+            pltpu.SemaphoreType.DMA((2, LEAPS)),
+            pltpu.SemaphoreType.DMA((2, NZL - 1, SLOTS)),
+            pltpu.SemaphoreType.DMA((2, 2, 11)),
+            pltpu.SemaphoreType.DMA((2,)),
+            pltpu.SemaphoreType.DMA((2,)),
+            pltpu.SemaphoreType.DMA((7,)),
+            pltpu.SemaphoreType.DMA((2, LEAPS)),
+            pltpu.SemaphoreType.DMA((2, NZL - 1)),
         ],
         compiler_params=pltpu.CompilerParams(collective_id=collective_id, has_side_effects=True, vmem_limit_bytes=48 << 20),
         name=name,

time: 86.8 us -> 83.6 us (0.963)
  Pallas kernels: 81.7 us -> 78.5 us
    pallas_call x1, Pallas kernels: 81.7 us -> 78.5 us  [square(): pl.pallas_call(kernel, out_shape=(jax.ShapeDtypeStruct((2, 1, SLOTS, B, B...]
where the time goes in v5:
time: 83.6 us; the launch traced here: 83.3 us
  Pallas kernels  78.5 us (94%)
  between operations  2.4 us (3%)
  local copies, waits for them, and re-layouts  1.68 us (2%)
    pallas_call x1, Pallas kernels, square(): pl.pallas_call(kernel, out_shape=(jax.ShapeDtypeStruct((2, 1, SLOTS, B, B...  78.5 us
    unnamed x3, local copies, waits for them, and re-layouts  1.68 us

profile of v5, /device:TPU:1, one launch (start us, length us, event | category | flops | bytes accessed | tf_op | source)
XLA Modules:
  0.0 83.3 jit_solution(5463314484825430248)
XLA Ops:
  0.6 0.7 select_bitcast_fusion.table
  1.4 0.0 copy-start
  1.4 1.0 %copy-done = f32[2,1,3,96,96]{4,3,2,1,0:T(8,128)S(1)} copy-done((f32[2,1,3,96,96]{4,3,2,1,0:T(8,128)S(1)}, f32[2,1,3,96,96]{4,3,2,1,0:T(8,128)}, u32[]{:S(2)}) %copy-start) | copy-done | bytes 221208
  2.3 78.5 %square.1 = (f32[2,1,3,96,96]{4,3,2,1,0:T(8,128)S(1)}, f32[1,1]{1,0:T(1,128)}) custom-call(s32[3072]{0:T(1024)S(1)} %select_bitcast_fusion.table, f32[2,1,3,96,96]{4,3,2,1,0:T(8,128)S(1)} %copy-done), custom_call_target="tpu_custom_call" | custom-call | tf_op jit(solution)/shard_map/square/pallas_call | solution.py:381
  80.8 0.7 copy.7
Async XLA Ops:
  1.4 1.0 %copy-start = (f32[2,1,3,96,96]{4,3,2,1,0:T(8,128)S(1)}, f32[2,1,3,96,96]{4,3,2,1,0:T(8,128)}, u32[]{:S(2)}) copy-start(f32[2,1,3,96,96]{4,3,2,1,0:T(8,128)} %b_ref.1) | copy-start | bytes 663556

commit v6 on v5

--- a/solution.py
+++ b/solution.py
@@ -10,7 +10,8 @@
 MESH = pl.DeviceIdType.MESH
 NX, NY, NZH, NZL, NK = 4, 4, 2, 8, 2
 NZ = NZH * NZL
-LEAPS = NZL // 2
+STRIDE = 2
+LEAPS = NZL // STRIDE
 B, SLOTS, PACK = 96, 3, 72
 CUT = 32
 NB, GROUPS, WIDTH = 128, 8, 16
@@ -18,7 +19,7 @@
 DEPTH = QUAD * SLOTS * 128
 
 T_RING, T_OWN, T_TAIL0, T_TAIL, T_SIDE0, T_SIDE, T_FAR = 3.6, 13.0, 14.0, 3.0, 18.0, 2.0, 16.0
-AT_NEAR, AT_TRACE, AT_LEFT = 24.5, 30.0, 37.0
+AT_NEAR, AT_TRACE, AT_LEFT = 28.0, 32.0, 37.0
 
 
 def here():
@@ -61,7 +62,7 @@
     return high, (value - high.astype(jnp.float32)).astype(jnp.bfloat16)
 
 
-def kernel(table, b_ref, out_ref, trace_ref, raw, own, line, near, far, lhs, rhs_hi, rhs_lo, in_plane, along, one, two, near_sum,
+def kernel(table, b_ref, out_ref, trace_ref, own, line, near, far, lhs, rhs_hi, rhs_lo, in_plane, along, one, two, near_sum,
            ruler,
            lsem, ring_in, side_in, tail_in, plane_in, share_in, small_in, out_sem, side_out, tail_out):
     me = here()
@@ -75,16 +76,13 @@
     barrier = pltpu.get_barrier_semaphore()
     for step in steps:
         pl.semaphore_signal(barrier, inc=1, device_id=ids[step], device_id_type=MESH)
-    load = pltpu.make_async_copy(b_ref, raw, lsem.at[0])
-    load.start()
-    load.wait()
     for i in range(2):
         for s in range(SLOTS):
-            own[i, s] = pack(raw[i, 0, s])
+            own[i, s] = pack(b_ref[i, 0, s])
     local = [
-        pltpu.make_async_copy(own, line.at[z], lsem.at[1]),
-        pltpu.make_async_copy(own.at[0], near.at[0, k, x, y], lsem.at[2]),
-        pltpu.make_async_copy(own.at[1], near.at[1, k, x, y], lsem.at[3]),
+        pltpu.make_async_copy(own, line.at[z], lsem.at[0]),
+        pltpu.make_async_copy(own.at[0], near.at[0, k, x, y], lsem.at[1]),
+        pltpu.make_async_copy(own.at[1], near.at[1, k, x, y], lsem.at[2]),
     ]
     for copy in local:
         copy.start()
@@ -116,13 +114,13 @@
 
     def ring_step(d, m, c):
         way = 1 - 2 * d
-        origin = ups[-way * 2 * m % NZ]
+        origin = ups[-way * STRIDE * m % NZ]
         if m > 0:
             ring[d, m - 1, c].wait_recv()
         if m < LEAPS:
             src = own.at[d, c] if m == 0 else line.at[origin, d, c]
             dst = line.at[origin, d, c] if m < LEAPS - 1 else far.at[d, k, x, y, c]
-            ring[d, m, c] = send(src, dst, ("z", 2 * way), out_sem.at[0], ring_in.at[d, m, c])
+            ring[d, m, c] = send(src, dst, ("z", STRIDE * way), out_sem.at[0], ring_in.at[d, m, c])
 
     def side_send(d, m, c):
         way = 1 - 2 * d
@@ -156,10 +154,12 @@
     for c in range(SLOTS):
         for d in range(2):
             for m in range(LEAPS):
-                events.append((T_RING * m + 0.76 * c, functools.partial(ring_step, d, m, c)))
-                events.append((T_SIDE0 + T_SIDE * m + 0.76 * c, functools.partial(side_send, d, m, c)))
+                if m > 0:
+                    events.append((T_RING * m + 0.76 * c, functools.partial(ring_step, d, m, c)))
+                at = T_SIDE0 + T_SIDE * m + 0.76 * c
+                events.append((at, functools.partial(side_send, d, m, c)))
                 if c == SLOTS - 1:
-                    events.append((T_SIDE0 + T_SIDE * m + 8.0 + 0.76 * c, functools.partial(side_wait, d, m)))
+                    events.append((at + 8.0, functools.partial(side_wait, d, m)))
             for n in range(NZL):
                 events.append((T_OWN if n == 0 else T_TAIL0 + T_TAIL * n + 0.76 * c, functools.partial(tail_step, d, n, c)))
 
@@ -190,11 +190,14 @@
             if phase == 1:
                 for c in range(SLOTS):
                     ring_step(ab, LEAPS, c)
-            for d, way in enumerate((1, -1, 2)):
+            for d, way in enumerate((1, -1)):
                 go(ab, me[a], me[second[ab]], a, way, d)
 
         def pass_on(ab, d):
             drain(plane_in.at[phase, ab, d], three)
+            if d < 2:
+                a, way = first[ab], 1 - 2 * d
+                go(ab, spot(a, -way), me[second[ab]], a, way, 2, d)
             spread(ab, (3, 1, 2)[d])
 
         def pass_second(ab, j):
@@ -202,12 +205,20 @@
             drain(plane_in.at[phase, ab, 3 + j], six)
             for d, way in enumerate((1, -1)):
                 go(ab, spot(a, j), spot(b, -way), b, way, 7 + j, d)
+            if phase == 1 and j == 2:
+                for by in (0, 1, 3):
+                    give(ref(ab, spot(a, j), spot(b, by)))
+
+        def give(view):
+            send(view, view, ("k", 1), out_sem.at[3 + phase], share_in.at[phase])
 
         def share(ab, j):
             drain(plane_in.at[phase, ab, 7 + j], three)
             p = spot(first[ab], j)
-            src = store.at[ab, k, p] if ab == 0 else store.at[ab, k, :, p]
-            send(src, src, ("k", 1), out_sem.at[3 + phase], share_in.at[phase])
+            if phase == 1 and j == 2:
+                give(ref(ab, p, spot(second[ab], 2)))
+                return
+            give(store.at[ab, k, p] if ab == 0 else store.at[ab, k, :, p])
 
         order = [
             (0.0, begin), (0.01, lambda ab: spread(ab, 0)),
@@ -224,6 +235,9 @@
         after.append((out_sem.at[1 + phase], line.at[pl.ds(0, 15)], None))
         after.append((out_sem.at[3 + phase], line, None))
 
+    for c in range(SLOTS):
+        for d in range(2):
+            ring_step(d, 0, c)
     for copy in local:
         copy.wait()
     plane(0, near, 0.0)
@@ -381,10 +395,9 @@
     return pl.pallas_call(
         kernel,
         out_shape=(jax.ShapeDtypeStruct((2, 1, SLOTS, B, B), jnp.float32), jax.ShapeDtypeStruct((1, 1), jnp.float32)),
-        in_specs=[pl.BlockSpec(memory_space=pltpu.SMEM), pl.BlockSpec(memory_space=pl.ANY)],
+        in_specs=[pl.BlockSpec(memory_space=pltpu.SMEM), pl.BlockSpec(memory_space=pltpu.VMEM)],
         out_specs=(pl.BlockSpec(memory_space=pltpu.VMEM), pl.BlockSpec(memory_space=pltpu.SMEM)),
         scratch_shapes=[
-            pltpu.VMEM((2, 1, SLOTS, B, B), jnp.float32),
             pltpu.VMEM((2, SLOTS, PACK, 128), jnp.float32),
             pltpu.VMEM((NZ, 2, SLOTS, PACK, 128), jnp.float32),
             pltpu.VMEM((2, NK, NX, NY, SLOTS, PACK, 128), jnp.float32),
@@ -398,7 +411,7 @@
             pltpu.VMEM((8, 128), jnp.float32),
             pltpu.VMEM((8, 128), jnp.float32),
             pltpu.VMEM((NX * NY * NK, 8, 128), jnp.float32),
-            pltpu.SemaphoreType.DMA((4,)),
+            pltpu.SemaphoreType.DMA((3,)),
             pltpu.SemaphoreType.DMA((2, LEAPS, SLOTS)),
             pltpu.SemaphoreType.DMA((2, LEAPS)),
             pltpu.SemaphoreType.DMA((2, NZL - 1, SLOTS)),

time: 83.6 us -> 80.9 us (0.968)
  Pallas kernels: 78.5 us -> 75.8 us
    pallas_call x1, Pallas kernels: 78.5 us -> 75.8 us  [square(): pl.pallas_call(kernel, out_shape=(jax.ShapeDtypeStruct((2, 1, SLOTS, B, B...]
where the time goes in v6:
time: 80.9 us; the launch traced here: 80.6 us
  Pallas kernels  75.8 us (94%)
  between operations  2.4 us (3%)
  local copies, waits for them, and re-layouts  1.68 us (2%)
    pallas_call x1, Pallas kernels, square(): pl.pallas_call(kernel, out_shape=(jax.ShapeDtypeStruct((2, 1, SLOTS, B, B...  75.8 us
    unnamed x3, local copies, waits for them, and re-layouts  1.68 us

profile of v6, /device:TPU:1, one launch (start us, length us, event | category | flops | bytes accessed | tf_op | source)
XLA Modules:
  0.0 80.6 jit_solution(4816306574232405282)
XLA Ops:
  0.6 0.7 select_bitcast_fusion.table
  1.4 0.0 copy-start
  1.4 1.0 %copy-done = f32[2,1,3,96,96]{4,3,2,1,0:T(8,128)S(1)} copy-done((f32[2,1,3,96,96]{4,3,2,1,0:T(8,128)S(1)}, f32[2,1,3,96,96]{4,3,2,1,0:T(8,128)}, u32[]{:S(2)}) %copy-start) | copy-done | bytes 221208
  2.3 75.8 %square.1 = (f32[2,1,3,96,96]{4,3,2,1,0:T(8,128)S(1)}, f32[1,1]{1,0:T(1,128)}) custom-call(s32[3072]{0:T(1024)S(1)} %select_bitcast_fusion.table, f32[2,1,3,96,96]{4,3,2,1,0:T(8,128)S(1)} %copy-done), custom_call_target="tpu_custom_call" | custom-call | tf_op jit(solution)/shard_map/square/pallas_call | solution.py:395
  78.2 0.7 copy.7
Async XLA Ops:
  1.4 1.0 %copy-start = (f32[2,1,3,96,96]{4,3,2,1,0:T(8,128)S(1)}, f32[2,1,3,96,96]{4,3,2,1,0:T(8,128)}, u32[]{:S(2)}) copy-start(f32[2,1,3,96,96]{4,3,2,1,0:T(8,128)} %b_ref.1) | copy-start | bytes 663556

commit v7 on v6

--- a/solution.py
+++ b/solution.py
@@ -18,8 +18,8 @@
 QUAD = GROUPS // NZH
 DEPTH = QUAD * SLOTS * 128
 
-T_RING, T_OWN, T_TAIL0, T_TAIL, T_SIDE0, T_SIDE, T_FAR = 3.6, 13.0, 14.0, 3.0, 18.0, 2.0, 16.0
-AT_NEAR, AT_TRACE, AT_LEFT = 28.0, 32.0, 37.0
+T_RING, T_OWN, T_TAIL0, T_TAIL, T_SIDE0, T_SIDE, T_FAR = 3.6, 15.0, 15.5, 3.0, 19.0, 2.0, 16.0
+AT_NEAR, AT_TRACE, AT_LEFT = 28.0, 32.0, 39.0
 
 
 def here():
@@ -276,7 +276,7 @@
                 rhs_hi[i, half, depth, s * 128:s * 128 + B] = high
                 rhs_lo[i, half, depth, s * 128:s * 128 + B] = low
 
-    def multiply(slots, i, half):
+    def multiply(slots, i, half, added=()):
         dot = functools.partial(jnp.dot, preferred_element_type=jnp.float32)
         lanes = slice(slots[0] * 128, (slots[-1] + 1) * 128)
         main = dot(lhs[i, half], rhs_hi[i, half, :, lanes])
@@ -284,10 +284,10 @@
         value = main[0:B] + (main[B:] + rest)
         for n, s in enumerate(slots):
             part = value[:, n * 128:n * 128 + B]
-            if half == 0:
+            if s in added:
+                out_ref[i, 0, s] += part
+            else:
                 out_ref[i, 0, s] = part
-            else:
-                out_ref[i, 0, s] += part
 
     def prepare():
         for ref in (rhs_hi, rhs_lo):
@@ -358,26 +358,25 @@
     events.append((AT_NEAR, lambda: every(functools.partial(right_side, whole), 0, zh)))
     events.append((AT_TRACE, early_trace))
     events.append((AT_TRACE + 3.0, lambda: pl.when(jnp.logical_and(holds, zh == 1))(to_line)))
-    events.append((AT_LEFT, lambda: every(left_side, 0, zh)))
-    events.append((AT_LEFT + 0.5, lambda: every(left_side, 1, other)))
-    for i in range(2):
-        events.append((AT_LEFT + 1.0 + i, functools.partial(multiply, whole, i, 0)))
+    events.append((AT_LEFT, lambda: every(left_side, 1, other)))
     for _, step in sorted(events, key=lambda e: e[0]):
         step()
 
-    def far_products(slots):
-        every(functools.partial(right_side, slots), 1, other)
-        for i in range(2):
-            multiply(slots, i, 1)
-
-    far_products(first)
+    every(functools.partial(right_side, first), 1, other)
+    for i in range(2):
+        multiply(first, i, 1)
 
     @pl.when(jnp.logical_and(diagonal, zh == 0))
     def _():
-        one[...] = 2.0 * diagonal_sum() - near_sum[...]
+        one[...] = 2.0 * diagonal_sum() + near_sum[...]
         to_plane()
 
-    far_products(rest)
+    every(left_side, 0, zh)
+    for i in range(2):
+        multiply(whole, i, 0, added=first)
+    every(functools.partial(right_side, rest), 1, other)
+    for i in range(2):
+        multiply(rest, i, 1, added=rest)
     pl.when(jnp.logical_and(holds, zh == 0))(to_line)
 
     drain(small_in.at[1], ruler.at[pl.ds(0, NZL)], jnp.logical_not(holds))

time: 80.9 us -> 80.8 us (level)
  no operation moved by 1% of the time
where the time goes in v7:
time: 80.8 us; the launch traced here: 80.5 us
  Pallas kernels  75.7 us (94%)
  between operations  2.4 us (3%)
  local copies, waits for them, and re-layouts  1.68 us (2%)
    pallas_call x1, Pallas kernels, square(): pl.pallas_call(kernel, out_shape=(jax.ShapeDtypeStruct((2, 1, SLOTS, B, B...  75.7 us
    unnamed x3, local copies, waits for them, and re-layouts  1.68 us

profile of v7, /device:TPU:1, one launch (start us, length us, event | category | flops | bytes accessed | tf_op | source)
XLA Modules:
  0.0 80.5 jit_solution(2799344986424634688)
XLA Ops:
  0.6 0.7 select_bitcast_fusion.table
  1.4 0.0 copy-start
  1.4 1.0 %copy-done = f32[2,1,3,96,96]{4,3,2,1,0:T(8,128)S(1)} copy-done((f32[2,1,3,96,96]{4,3,2,1,0:T(8,128)S(1)}, f32[2,1,3,96,96]{4,3,2,1,0:T(8,128)}, u32[]{:S(2)}) %copy-start) | copy-done | bytes 221208
  2.3 75.7 %square.1 = (f32[2,1,3,96,96]{4,3,2,1,0:T(8,128)S(1)}, f32[1,1]{1,0:T(1,128)}) custom-call(s32[3072]{0:T(1024)S(1)} %select_bitcast_fusion.table, f32[2,1,3,96,96]{4,3,2,1,0:T(8,128)S(1)} %copy-done), custom_call_target="tpu_custom_call" | custom-call | tf_op jit(solution)/shard_map/square/pallas_call | solution.py:394
  78.1 0.7 copy.7
Async XLA Ops:
  1.4 1.0 %copy-start = (f32[2,1,3,96,96]{4,3,2,1,0:T(8,128)S(1)}, f32[2,1,3,96,96]{4,3,2,1,0:T(8,128)}, u32[]{:S(2)}) copy-start(f32[2,1,3,96,96]{4,3,2,1,0:T(8,128)} %b_ref.1) | copy-start | bytes 663556

commit v8 on v7

--- a/solution.py
+++ b/solution.py
@@ -205,7 +205,7 @@
             drain(plane_in.at[phase, ab, 3 + j], six)
             for d, way in enumerate((1, -1)):
                 go(ab, spot(a, j), spot(b, -way), b, way, 7 + j, d)
-            if phase == 1 and j == 2:
+            if phase == 1 and j in (1, 2):
                 for by in (0, 1, 3):
                     give(ref(ab, spot(a, j), spot(b, by)))
 
@@ -215,7 +215,7 @@
         def share(ab, j):
             drain(plane_in.at[phase, ab, 7 + j], three)
             p = spot(first[ab], j)
-            if phase == 1 and j == 2:
+            if phase == 1 and j in (1, 2):
                 give(ref(ab, p, spot(second[ab], 2)))
                 return
             give(store.at[ab, k, p] if ab == 0 else store.at[ab, k, :, p])

time: 80.8 us -> 80.8 us (level)
  no operation moved by 1% of the time
where the time goes in v8:
time: 80.8 us; the launch traced here: 80.5 us
  Pallas kernels  75.7 us (94%)
  between operations  2.4 us (3%)
  local copies, waits for them, and re-layouts  1.68 us (2%)
    pallas_call x1, Pallas kernels, square(): pl.pallas_call(kernel, out_shape=(jax.ShapeDtypeStruct((2, 1, SLOTS, B, B...  75.7 us
    unnamed x3, local copies, waits for them, and re-layouts  1.68 us

profile of v8, /device:TPU:1, one launch (start us, length us, event | category | flops | bytes accessed | tf_op | source)
XLA Modules:
  0.0 80.5 jit_solution(10970999842472476987)
XLA Ops:
  0.6 0.7 select_bitcast_fusion.table
  1.4 0.0 copy-start
  1.4 1.0 %copy-done = f32[2,1,3,96,96]{4,3,2,1,0:T(8,128)S(1)} copy-done((f32[2,1,3,96,96]{4,3,2,1,0:T(8,128)S(1)}, f32[2,1,3,96,96]{4,3,2,1,0:T(8,128)}, u32[]{:S(2)}) %copy-start) | copy-done | bytes 221208
  2.3 75.7 %square.1 = (f32[2,1,3,96,96]{4,3,2,1,0:T(8,128)S(1)}, f32[1,1]{1,0:T(1,128)}) custom-call(s32[3072]{0:T(1024)S(1)} %select_bitcast_fusion.table, f32[2,1,3,96,96]{4,3,2,1,0:T(8,128)S(1)} %copy-done), custom_call_target="tpu_custom_call" | custom-call | tf_op jit(solution)/shard_map/square/pallas_call | solution.py:394
  78.1 0.7 copy.7
Async XLA Ops:
  1.4 1.0 %copy-start = (f32[2,1,3,96,96]{4,3,2,1,0:T(8,128)S(1)}, f32[2,1,3,96,96]{4,3,2,1,0:T(8,128)}, u32[]{:S(2)}) copy-start(f32[2,1,3,96,96]{4,3,2,1,0:T(8,128)} %b_ref.1) | copy-start | bytes 663556
